TPU v7x, 256 devices: a whole 4x4x8 slice. The times are simulated.
256 devices in a mesh: section: 4 (over x_hi, core), seq: 64 (over y, x_lo, z).
Axes of the slice: x: 4 (x_hi: 2, x_lo: 2; x = x_hi * 2 + x_lo), y: 4, z: 8, core: 2. Of those that a mesh axis runs over, the one named last changes fastest.
Arguments:
- hidden: bfloat16 [32768, 4096], P(('seq', 'section')), may hold values from -6 to 6
- norm_gain: float32 [4096], replicated, may hold values from 0.1 to 1.9
- w_query: bfloat16 [4096, 4096], P('seq', 'section'), may hold values from -0.09375 to 0.09375
- w_keyval: bfloat16 [2, 896, 4096], P(None, None, 'section'), may hold values from -120 to 120
- nbr_states: bfloat16 [512, 256, 896], P('seq'), may hold values from -24 to 24
- nbr_lens: int32 [512, 2], replicated, may hold values from 32 to 128
- segment_ids: int32 [32768], replicated, may hold values from 0 to 63, never falling along the last dimension, each value on 1 to 16384 neighbouring positions
Outputs:
- context: bfloat16 [32768, 4096], P('seq', 'section')
All inputs are finite; a program needn't handle non-finite values.
Results may differ from a plain program's by a relative error of at most 0.017.
The roundings to bfloat16 on the way count: a program that leaves them out, or rounds other values in their place, can miss the bound.
Values may be sent and summed in bfloat16 or wider, within the bound.
No kernel may reach another device: no remote copies, remote signals or barrier semaphores. Data moves between devices by JAX's collectives and lax.ppermute only.
A program may use at most 128 MiB of HBM per device.

v0:
```python
import jax
import jax.numpy as jnp
from jax import lax
from jax.sharding import PartitionSpec as P

HEAD_DIM = 128
SPAN = 64
NBR_LEN = 128


def from_behind(shard, axis, by):
    length = lax.axis_size(axis)
    pairs = [(i, i + by) for i in range(length) if 0 <= i + by < length]
    return lax.ppermute(shard, axis, pairs)


def normalize(source, norm_gain):
    values = source.astype(jnp.float32)
    factor = lax.rsqrt(jnp.mean(values * values, axis=-1, keepdims=True) + 1e-06)
    return (values * factor * norm_gain).astype(jnp.bfloat16)


def attend(query_blocks, key_blocks, value_blocks, key_lengths, live_rows):
    scores = jnp.einsum(
        "bqhd,bkhd->bhqk", query_blocks, key_blocks, preferred_element_type=jnp.float32
    )
    keys_total = key_blocks.shape[1]
    position = lax.broadcasted_iota(jnp.int32, (1, keys_total), 1) % NBR_LEN
    limits = jnp.repeat(key_lengths, NBR_LEN, axis=1)
    usable = (position < limits)[:, None, None, :]
    scores = jnp.where(usable, scores, jnp.float32(-1e30))
    highest = jnp.max(scores, axis=-1, keepdims=True)
    weights = jnp.where(usable, jnp.exp(scores - highest), jnp.float32(0.0))
    weights = (weights / jnp.sum(weights, axis=-1, keepdims=True)).astype(jnp.bfloat16)
    mixed = jnp.einsum("bhqk,bkhd->bqhd", weights, value_blocks, preferred_element_type=jnp.float32)
    mixed = mixed * live_rows[:, :, None, None].astype(jnp.float32)
    return mixed.astype(jnp.bfloat16)


def local(hidden, norm_gain, w_query, w_keyval, nbr_states, nbr_lens, segment_ids):
    normed = normalize(lax.all_gather(hidden, "section", axis=0, tiled=True), norm_gain)
    tok_rows = normed.shape[0]
    blocks = tok_rows // SPAN
    width = w_query.shape[1]
    heads_here = width // HEAD_DIM
    totals = jnp.dot(
        normed,
        lax.all_gather(w_query, "seq", axis=0, tiled=True),
        preferred_element_type=jnp.float32,
    )
    query = (totals * HEAD_DIM ** (-0.5)).astype(jnp.bfloat16)
    projected = jnp.einsum(
        "cne,kef->kcnf", nbr_states, w_keyval, preferred_element_type=jnp.float32
    ).astype(jnp.bfloat16)
    prev_keys, prev_values = from_behind((projected[0, -1], projected[1, -1]), "seq", 1)
    neighbour_rows = projected.shape[2]
    key_blocks = jnp.concatenate([prev_keys[None], projected[0]], axis=0).reshape(
        blocks + 1, neighbour_rows, heads_here, HEAD_DIM
    )
    value_blocks = jnp.concatenate([prev_values[None], projected[1]], axis=0).reshape(
        blocks + 1, neighbour_rows, heads_here, HEAD_DIM
    )
    query_padded = jnp.concatenate(
        [jnp.zeros((1, width), jnp.bfloat16), query, jnp.zeros((SPAN - 1, width), jnp.bfloat16)],
        axis=0,
    )
    query_blocks = query_padded.reshape(blocks + 1, SPAN, heads_here, HEAD_DIM)
    first_span = lax.axis_index("seq") * blocks
    padded_lengths = jnp.concatenate(
        [jnp.ones((1, nbr_lens.shape[1]), jnp.int32), nbr_lens], axis=0
    )
    key_lengths = lax.dynamic_slice_in_dim(padded_lengths, first_span, blocks + 1, 0)
    first_token = first_span * SPAN
    own_segments = lax.dynamic_slice_in_dim(segment_ids, first_token, tok_rows, 0)
    row_segments = jnp.concatenate(
        [jnp.full((1,), -1, jnp.int32), own_segments, jnp.full((SPAN - 1,), -1, jnp.int32)]
    ).reshape(blocks + 1, SPAN)
    shifted_ids = jnp.concatenate([jnp.full((1,), -2, jnp.int32), segment_ids])
    end_segments = lax.dynamic_slice_in_dim(shifted_ids, first_token, blocks * SPAN + 1, 0)[::SPAN]
    live_rows = row_segments == end_segments[:, None]
    mixed = attend(query_blocks, key_blocks, value_blocks, key_lengths, live_rows)
    return mixed.reshape((blocks + 1) * SPAN, width)[1 : 1 + tok_rows]


def solution(mesh):
    in_specs = (
        P(("seq", "section"), None),
        P(),
        P("seq", "section"),
        P(None, None, "section"),
        P("seq", None, None),
        P(),
        P(),
    )
    out_specs = P("seq", "section")
    return jax.shard_map(local, mesh=mesh, in_specs=in_specs, out_specs=out_specs, check_vma=False)
```

profile of v0, /device:TPU:4, one launch (start us, length us, event | category | flops | bytes accessed | tf_op | source)
XLA Modules:
  0.0 409.8 jit_solution(16613672629423841127)
XLA Ops:
  6.5 0.7 all-gather.3.cloned.1.call-update
  7.3 0.7 all-gather.5.cloned.1.call-update
  8.0 11.9 %convert_bitcast_fusion = bf16[2,8,256,1024]{2,3,1,0:T(8,128)(2,1)S(1)} fusion(bf16[2,896,1024]{2,1,0:T(8,128)(2,1)} %param.10, bf16[8,256,896]{2,1,0:T(8,128)(2,1)} %param.11), kind=kOutput, calls=%fused_computation.6 | convolution fusion | flops 7520387072 | bytes 15728640 | tf_op jit(solution)/shard_map/cne,kef->kcnf/dot_general | solution.py:52
  19.9 3.2 copy-done.1
  23.2 3.8 collective-permute-start.1
  27.1 4.0 collective-permute-start
  31.9 5.8 %fusion.36 = (bf16[1,8,256,1024]{2,3,1,0:T(8,128)(2,1)}, bf16[1,8,256,1024]{2,3,1,0:T(8,128)(2,1)}) fusion(bf16[2,8,256,1024]{2,3,1,0:T(8,128)(2,1)} %copy-done.1), kind=kLoop, calls=%fused_computation.46 | loop fusion | bytes 16777216 | tf_op jit(solution)/shard_map/slice | solution.py:57
  37.7 6.4 %copy.20 = bf16[8,256,8,128]{3,1,2,0:T(8,128)(2,1)} copy(bf16[8,256,8,128]{1,3,2,0:T(8,128)(2,1)} %bitcast.35) | data formatting | bytes 8388608 | tf_op jit(solution)/shard_map/concatenate | solution.py:57
  44.1 6.5 %copy.17 = bf16[8,256,8,128]{3,1,2,0:T(8,128)(2,1)} copy(bf16[8,256,8,128]{1,3,2,0:T(8,128)(2,1)} %bitcast.34) | data formatting | bytes 8388608 | tf_op jit(solution)/shard_map/concatenate | solution.py:60
  50.7 0.3 copy.19
  50.9 0.3 copy.16
  51.2 21.8 %all-gather.3.cloned.1.call-done = bf16[512,4096]{1,0:T(8,128)(2,1)} async-done(((bf16[128,4096]{1,0:T(8,128)(2,1)}), bf16[512,4096]{1,0:T(8,128)(2,1)}) %all-gather.3.cloned.1.call-update) | async-done | bytes 4194320 | tf_op jit(solution)/shard_map/all_gather | solution.py:41
  73.0 3.1 fusion.1
  76.1 307.3 %all-gather.5.cloned.1.call-done = bf16[4096,1024]{1,0:T(8,128)(2,1)} async-done(((bf16[64,1024]{1,0:T(8,128)(2,1)}), bf16[4096,1024]{1,0:T(8,128)(2,1)}) %all-gather.5.cloned.1.call-update) | async-done | bytes 8388624 | tf_op jit(solution)/shard_map/all_gather | solution.py:48
  383.4 9.2 %multiply_convert_fusion.1 = bf16[512,1024]{1,0:T(8,128)(2,1)S(1)} fusion(bf16[4096,1024]{1,0:T(8,128)(2,1)} %all-gather.5.cloned.1.call-done, bf16[512,4096]{1,0:T(8,128)(2,1)} %all-gather.3.cloned.1.call-done, f32[4096]{0:T(1024)S(1)} %copy-done.5, f32[512]{0:T(512)S(1)} %add_rsqrt_fusion), kind=kOutput, calls=%fused_computation.28 | convolution fusion | flops 4304404480 | bytes 13649920 | tf_op jit(solution)/shard_map/dot_general | solution.py:46
  392.6 0.5 maximum_bitcast_fusion
  393.1 0.3 copy.27
  393.4 1.4 copy-done
  394.8 1.7 fusion.4
  396.5 2.3 fusion.37
  398.9 1.7 fusion.28
  400.6 0.8 copy.22
  401.4 0.3 copy.32
  401.7 1.3 slice.28
  (33 shorter events, 1.0 us)
Async XLA Ops:
  6.5 66.5 %all-gather.3.cloned.1.call-start = ((), (), s32[]{:S(2)}) async-start(), calls=%async_computation | async-start | bytes 5242880 | tf_op jit(solution)/shard_map/all_gather | solution.py:41
  7.3 376.1 %all-gather.5.cloned.1.call-start = ((), (), s32[]{:S(2)}) async-start(), calls=%async_computation.1 | async-start | bytes 8519680 | tf_op jit(solution)/shard_map/all_gather | solution.py:48
  8.0 23.2 %copy-start.3 = (s32[32768]{0:T(1024)S(1)}, s32[32768]{0:T(1024)}, u32[]{:S(2)}) copy-start(s32[32768]{0:T(1024)} %param.13) | copy-start | bytes 393220
  8.0 23.6 %copy-start.4 = (s32[512,2]{0,1:T(2,128)S(1)}, s32[512,2]{0,1:T(2,128)}, u32[]{:S(2)}) copy-start(s32[512,2]{0,1:T(2,128)} %param.12) | copy-start | bytes 12292
  19.9 3.2 copy-start.1
  23.2 27.5 %collective-permute-start.1 = (bf16[256,1024]{0,1:T(8,128)(2,1)S(1)}, bf16[256,1024]{0,1:T(8,128)(2,1)S(1)}, u32[]{:S(2)}, u32[]{:S(2)}) collective-permute-start(bf16[256,1024]{0,1:T(8,128)(2,1)S(1)} %get-tuple-element.5), channel_id=1, source_target_pairs={{0,1},{1,2},{2,3},{3,4},{4,5},{5,6},{6,7},{7,8},{8,9},{9,10},{10,1... | collective-permute-start | bytes 1572872 | tf_op jit(solution)/shard_map/ppermute | solution.py:14
  27.1 23.9 %collective-permute-start = (bf16[256,1024]{0,1:T(8,128)(2,1)S(1)}, bf16[256,1024]{0,1:T(8,128)(2,1)S(1)}, u32[]{:S(2)}, u32[]{:S(2)}) collective-permute-start(bf16[256,1024]{0,1:T(8,128)(2,1)S(1)} %get-tuple-element.6), channel_id=1, source_target_pairs={{0,1},{1,2},{2,3},{3,4},{4,5},{5,6},{6,7},{7,8},{8,9},{9,10},{10,1... | collective-permute-start | bytes 1572872 | tf_op jit(solution)/shard_map/ppermute | solution.py:14
  50.6 332.8 %copy-start.5 = (f32[4096]{0:T(1024)S(1)}, f32[4096]{0:T(1024)}, u32[]{:S(2)}) copy-start(f32[4096]{0:T(1024)} %param.8) | copy-start | bytes 49156
  392.6 2.2 copy-start
  396.5 2.3 copy-start.2
Sparse Core Ops, SparseCore 0:
  9.2 63.7 all-gather.2
  74.8 308.5 all-gather.4
where the time goes:
time: 410 us
  waiting for transfers between devices  330 us (80%)
  local copies, waits for them, and re-layouts  27.2 us (7%)
  matrix products  24.5 us (6%)
  between operations  13.6 us (3%)
  starting transfers between devices  7.9 us (2%)
  other arithmetic  6.12 us (1%)
    all_gather x1, waiting for transfers between devices, local(): lax.all_gather(w_query, 'seq', axis=0, tiled=True)  307 us
    all_gather x1, waiting for transfers between devices, local(): lax.all_gather(hidden, 'section', axis=0, tiled=True)  21.8 us
    dot_general x1, matrix products, local(): jnp.einsum('cne,kef->kcnf', nbr_states, w_keyval, preferred_element_type=...  11.9 us
    dot_general x1, matrix products, local(): jnp.dot(normed, lax.all_gather(w_query, 'seq', axis=0, tiled=True), prefe...  9.19 us
  transfers between devices with their start and end apart: 4, of which 2 were waited for; matrix products, arithmetic and copies ran while one was open for 9% of the time, Pallas kernels for 0%

commit v1 on v0

v1 whole, which is shorter than its diff:
```python
import jax
import jax.numpy as jnp
from jax import lax
from jax.experimental import pallas as pl
from jax.experimental.pallas import tpu as pltpu
from jax.sharding import Mesh, PartitionSpec as P

HEAD_DIM = 128
SPAN = 64
NBR_LEN = 128
SIZES = {"xh": 2, "core": 2, "y": 4, "xl": 2, "z": 8}
PLANE = ("core", "y", "xl", "z")
VMEM = pl.BlockSpec(memory_space=pltpu.VMEM)
SMEM = pl.BlockSpec(memory_space=pltpu.SMEM)
MIB = 1 << 20


def params(mib):
    return pltpu.CompilerParams(vmem_limit_bytes=mib * MIB)


def cost(flops, moved, exps=0):
    return pl.CostEstimate(flops=flops, bytes_accessed=moved, transcendentals=exps)


def place(w):
    return (w, 0) if w < 4 else (7 - w, 1)


def ring_pairs(by, inner):
    pairs = []
    for core in range(2):
        along_z = (core == 0) == inner
        for w in range(8):
            for z in range(8):
                w2, z2 = (w, (z + by) % 8) if along_z else ((w + by) % 8, z)
                (y, xl), (y2, xl2) = place(w), place(w2)
                pairs.append(
                    (((core * 4 + y) * 2 + xl) * 8 + z, ((core * 4 + y2) * 2 + xl2) * 8 + z2)
                )
    return pairs


def step(x, by, inner):
    return lax.ppermute(x, PLANE, ring_pairs(by, inner))


def hop(x, axis):
    return lax.ppermute(x, axis, [(0, 1), (1, 0)])


def slot_of(inner_axis_z, by):
    if inner_axis_z:
        return lax.rem(lax.axis_index("z") + by + 8, 8)
    y, xl = lax.axis_index("y"), lax.axis_index("xl")
    w = lax.rem(jnp.where(xl == 0, y, 7 - y) + by + 8, 8)
    return jnp.where(w < 4, 2 * w, 2 * (7 - w) + 1)


INNER = (0, -1, 1, -2, 2, -3, 3, -4)


def stack_kernel(*refs):
    outs, rows, half = refs[8:], refs[0].shape[0], refs[8].shape[1]
    on_z = lax.axis_index("core") == 0
    for by, ref in zip(INNER, refs[:8], strict=True):
        slot = jnp.where(on_z, slot_of(True, by), slot_of(False, by))
        for i, out in enumerate(outs):
            out[pl.ds(pl.multiple_of(slot * rows, rows), rows), :] = ref[:, i * half : (i + 1) * half]


def stacked(parts):
    rows, columns = parts[0].shape
    shape = jax.ShapeDtypeStruct((8 * rows, columns // 2), parts[0].dtype)
    return pl.pallas_call(
        stack_kernel,
        out_shape=[shape, shape],
        in_specs=[VMEM] * 8,
        out_specs=[VMEM, VMEM],
        compiler_params=params(8),
        cost_estimate=cost(0, 32 * rows * columns),
        name="stack",
    )(*parts)


def norm_kernel(hidden_ref, gain_ref, out_ref):
    values = hidden_ref[...].astype(jnp.float32)
    factor = lax.rsqrt(jnp.mean(values * values, axis=-1, keepdims=True) + 1e-06)
    out_ref[...] = (values * factor * gain_ref[...]).astype(jnp.bfloat16)


def normalize(hidden, gain):
    rows, width = hidden.shape
    return pl.pallas_call(
        norm_kernel,
        out_shape=jax.ShapeDtypeStruct((rows, width), jnp.bfloat16),
        in_specs=[VMEM, VMEM],
        out_specs=VMEM,
        compiler_params=params(8),
        cost_estimate=cost(6 * rows * width, 4 * rows * width),
        name="norm",
    )(hidden, gain)


def rows_kernel(own_ref, near_ref, far_ref, far_near_ref, out):
    xh, core = lax.axis_index("xh"), lax.axis_index("core")
    slots = [xh * 2 + core, xh * 2 + 1 - core, 2 - 2 * xh + core, 3 - 2 * xh - core]
    refs = [own_ref, near_ref, far_ref, far_near_ref]
    rows = own_ref.shape[0]

    @pl.when(core == 0)
    def _():
        for slot, ref in zip(slots, refs, strict=True):
            out[pl.ds(pl.multiple_of(slot * rows, rows), rows), :] = ref[...]

    @pl.when(core == 1)
    def _():
        for slot, ref in zip(slots, refs, strict=True):
            at = pl.ds(pl.multiple_of(slot * rows, rows), rows)
            for z in range(8):
                for k in range(4):
                    one = ref[:, (16 * k + z) * 64 : (16 * k + z) * 64 + 64]
                    two = ref[:, (16 * k + 8 + z) * 64 : (16 * k + 8 + z) * 64 + 64]
                    to = z * 512 + k * 128
                    out[at, to : to + 128] = jnp.concatenate([one, two], axis=1)


def gather_rows(parts):
    rows, width = parts[0].shape
    return pl.pallas_call(
        rows_kernel,
        out_shape=jax.ShapeDtypeStruct((4 * rows, width), parts[0].dtype),
        in_specs=[VMEM] * 4,
        out_specs=VMEM,
        compiler_params=params(16),
        cost_estimate=cost(0, 16 * rows * width),
        name="rows",
    )(*parts)


def project_kernel(prev_ref, states_ref, w_ref, out_ref):
    for i in range(out_ref.shape[0]):
        block = prev_ref[0] if i == 0 else states_ref[i - 1]
        out_ref[i] = jnp.dot(block, w_ref[0], preferred_element_type=jnp.float32).astype(jnp.bfloat16)


def project(prev, states, w, which, half):
    spans, keys, depth = states.shape
    columns = w.shape[2] // 2
    whole = lambda i: (0, 0, 0)
    return pl.pallas_call(
        project_kernel,
        grid=(1,),
        out_shape=jax.ShapeDtypeStruct((spans + 1, keys, columns), jnp.bfloat16),
        in_specs=[
            pl.BlockSpec(prev.shape, whole, pipeline_mode=pl.Buffered(1)),
            pl.BlockSpec(states.shape, whole, pipeline_mode=pl.Buffered(1)),
            pl.BlockSpec((1, depth, columns), lambda i: (which, 0, half), pipeline_mode=pl.Buffered(1)),
        ],
        out_specs=pl.BlockSpec((spans + 1, keys, columns), whole, pipeline_mode=pl.Buffered(1)),
        compiler_params=params(20),
        cost_estimate=cost(2 * (spans + 1) * keys * depth * columns, 6 * MIB),
        name="project",
    )(prev, states, w)


def outer_slots(steps):
    on_z = lax.axis_index("core") == 1
    return [jnp.where(on_z, slot_of(True, by), slot_of(False, by)) for by in steps]


def products(n_ref, refs, places):
    total = None
    for ref, (slot, start) in zip(refs, places, strict=True):
        depth = ref.shape[0]
        lanes = pl.ds(pl.multiple_of(slot * 512 + start, 256), depth)
        term = jnp.dot(n_ref[:, lanes], ref[...], preferred_element_type=jnp.float32)
        total = term if total is None else total + term
    return total


def partial_product(n, steps, pieces, before=None):
    rows, columns = n.shape[0], pieces[0].shape[1]
    depth = sum(p.shape[0] for p in pieces)
    extra = [] if before is None else [before]

    def body(n_ref, *refs):
        places = [(slot, 0) for slot in outer_slots(steps)]
        total = products(n_ref, refs[: len(pieces)], places)
        if extra:
            total = total + refs[len(pieces)][...]
        refs[-1][...] = total

    return pl.pallas_call(
        body,
        out_shape=jax.ShapeDtypeStruct((rows, columns), jnp.float32),
        in_specs=[VMEM] * (1 + len(pieces) + len(extra)),
        out_specs=VMEM,
        compiler_params=params(20),
        cost_estimate=cost(2 * rows * depth * columns, 2 * depth * (rows + columns)),
        name="partial",
    )(n, *pieces, *extra)


def attend(lens, segments, total, n, steps, pieces, keys, values, other=None):
    rows, columns = total.shape
    blocks = keys.shape[0]
    heads = columns // HEAD_DIM
    extra = [] if other is None else [other]
    count = len(pieces)

    def body(lens_ref, seg_ref, total_ref, n_ref, k_ref, v_ref, *refs):
        piece_refs, (out_ref, q_scr, c_scr, s_scr, w_scr) = refs[:count], refs[-5:]
        if extra:
            out_ref[:, :columns] = refs[count][...]
        seq = (lax.axis_index("y") * 2 + lax.axis_index("xl")) * 8 + lax.axis_index("z")
        slots = outer_slots(steps)
        places = [(slot, 0) for slot in slots[:-1]] + [(slots[-1], 256)]
        acc = total_ref[...] + products(n_ref, piece_refs, places)
        acc = acc * HEAD_DIM ** (-0.5)
        acc = jnp.concatenate([acc, jnp.zeros((SPAN, columns), jnp.float32)], axis=0)
        q_scr[...] = pltpu.roll(acc, 1, 0).astype(jnp.bfloat16)
        lane = lax.broadcasted_iota(jnp.int32, (1, 128), 1)
        wide = lax.broadcasted_iota(jnp.int32, (1, 2 * NBR_LEN), 1)
        row = lax.broadcasted_iota(jnp.int32, (SPAN, HEAD_DIM), 0)
        usable, live = [], []
        for b in range(blocks):
            span = jnp.maximum(seq * (blocks - 1) + b - 1, 0)
            usable.append(
                wide < jnp.where(wide < NBR_LEN, lens_ref[0, span], lens_ref[1, span] + NBR_LEN)
            )
            line = seg_ref[pl.ds(span // 2, 1), :]
            if b % 2:
                same = (line == line[:, 63:64]) & (lane >= 63) & (lane < 127)
                number = jnp.sum(same.astype(jnp.int32), axis=1, keepdims=True)
            else:
                following = seg_ref[pl.ds(jnp.minimum(span // 2 + 1, seg_ref.shape[0] - 1), 1), :]
                same = (following == line[:, 127:128]) & (lane < 63)
                number = jnp.sum(same.astype(jnp.int32), axis=1, keepdims=True) + 1
            if b == 0:
                number = jnp.where(seq == 0, 0, number)
            live.append(row < number)
        for h in range(heads):
            at = slice(h * HEAD_DIM, (h + 1) * HEAD_DIM)
            for b in range(blocks):
                scores = lax.dot_general(
                    q_scr[b * SPAN : (b + 1) * SPAN, at],
                    k_ref[b, :, at],
                    (((1,), (1,)), ((), ())),
                    preferred_element_type=jnp.float32,
                )
                s_scr[h, b * SPAN : (b + 1) * SPAN, :] = jnp.where(usable[b], scores, jnp.float32(-1e30))
        for h in range(heads):
            for c in range(blocks // 3):
                r = slice(c * 3 * SPAN, (c + 1) * 3 * SPAN)
                scores = s_scr[h, r, :]
                weights = jnp.exp(scores - jnp.max(scores, axis=-1, keepdims=True))
                scale = 1.0 / jnp.sum(weights, axis=-1, keepdims=True)
                w_scr[h, r, :] = (weights * scale).astype(jnp.bfloat16)
        for h in range(heads):
            at = slice(h * HEAD_DIM, (h + 1) * HEAD_DIM)
            for b in range(blocks):
                mixed = jnp.dot(
                    w_scr[h, b * SPAN : (b + 1) * SPAN, :],
                    v_ref[b, :, at],
                    preferred_element_type=jnp.float32,
                )
                c_scr[b * SPAN : (b + 1) * SPAN, at] = jnp.where(live[b], mixed, 0.0)
        moved = pltpu.roll(c_scr[...], blocks * SPAN - 1, 0)
        out_ref[:, len(extra) * columns :] = moved[:rows].astype(jnp.bfloat16)

    return pl.pallas_call(
        body,
        out_shape=jax.ShapeDtypeStruct((rows, columns * (1 + len(extra))), jnp.bfloat16),
        in_specs=[SMEM] + [VMEM] * (5 + count + len(extra)),
        out_specs=VMEM,
        scratch_shapes=[
            pltpu.VMEM((blocks * SPAN, columns), jnp.bfloat16),
            pltpu.VMEM((blocks * SPAN, columns), jnp.float32),
            pltpu.VMEM((heads, blocks * SPAN, 2 * NBR_LEN), jnp.float32),
            pltpu.VMEM((heads, blocks * SPAN, 2 * NBR_LEN), jnp.bfloat16),
        ],
        compiler_params=params(28),
        cost_estimate=cost(3 * MIB * 1000, 8 * MIB),
        name="attend",
    )(lens, segments, total, n, keys, values, *pieces, *extra)


def after(value, *others):
    return lax.optimization_barrier((value, *others))[0]


def local(hidden, norm_gain, w_query, w_keyval, nbr_states, nbr_lens, segment_ids):
    a, b = step(w_query, 1, True), step(w_query, -1, True)
    normed = normalize(hidden, norm_gain[None])
    far = hop(normed, "xh")
    near = hop(normed, "core")
    inner = [w_query, a, b]
    a, b = step(after(a, normed), 1, True), step(after(b, normed), -1, True)
    inner += [a, b]
    prev = lax.ppermute(after(nbr_states[-1:], a, b), ("y", "xl", "z"), [(i, i + 1) for i in range(63)])
    a, b = step(after(a, near), 1, True), step(after(b, near), -1, True)
    inner += [a, b]
    inner.append(step(b, -1, True))
    columns = stacked(inner)

    def projected(which, part, *first):
        return project(prev, after(nbr_states, *first), w_keyval, which, part)

    def both(pair, *first):
        a, b = pair
        return step(after(a, *first), 1, False), step(after(b, *first), -1, False)

    one = [(columns[0], columns[0])]
    two = [(columns[1], columns[1])]
    one.append(both(one[0]))
    two.append(both(two[0]))
    far_near = hop(after(far, *columns), "core")
    keys_a = projected(0, 0, *columns)
    values_a = projected(1, 0, keys_a)
    one.append(both(one[1], values_a))
    keys_b = projected(0, 1, *one[1])
    two.append(both(two[1], keys_b))
    values_b = projected(1, 1, *two[1])
    one.append(both(one[2], values_b, far_near))
    whole = gather_rows([after(normed, *one[2]), near, far, far_near])
    total_a = partial_product(whole, [0, -1, 1], [columns[0], *one[1]])
    two.append(both(two[2], total_a))
    total_b = partial_product(whole, [0, -1, 1], [columns[1], *two[1]])
    total_a = partial_product(whole, [-2, 2], one[2], total_a)

    def split(pair, *first):
        a, b = pair
        r = a.shape[0] // 2
        return step(after(a[:r], *first), 1, False), step(after(b[r:], *first), -1, False)

    one.append(split(one[3], total_a, total_b))
    total_b = partial_product(whole, [-2, 2], two[2], after(total_b, *one[3]))
    two.append(split(two[3], total_b))
    total_a = partial_product(whole, [-3, 3], one[3], after(total_a, *two[3]))
    lens, segments = nbr_lens.T, segment_ids.reshape(-1, 128)
    out = attend(lens, segments, total_a, whole, [-4, -4], one[4], keys_a, values_a)
    total_b = partial_product(whole, [-3, 3], two[3], after(total_b, out))
    return attend(lens, segments, total_b, whole, [-4, -4], two[4], keys_b, values_b, out)


def solution(mesh):
    fine = Mesh(mesh.devices.reshape(tuple(SIZES.values())), tuple(SIZES))
    section, seq = ("xh", "core"), ("y", "xl", "z")
    in_specs = (
        P(seq + section, None),
        P(),
        P(seq, section),
        P(None, None, section),
        P(seq, None, None),
        P(),
        P(),
    )
    out_specs = P(seq, section)
    return jax.shard_map(local, mesh=fine, in_specs=in_specs, out_specs=out_specs, check_vma=False)
```

time: 410 us -> 108 us (0.26)
  the two profiles are of different devices: /device:TPU:4 before, /device:TPU:2 now
where the time goes in v1:
time: 108 us; the launch traced here: 107 us
  starting transfers between devices  60 us (56%)
  Pallas kernels  22.2 us (21%)
  waiting for transfers between devices  18 us (17%)
  local copies, waits for them, and re-layouts  6.22 us (6%)
    ppermute x23, starting transfers between devices, step(): return lax.ppermute(x, PLANE, ring_pairs(by, inner))  34.6 us
    ppermute x3, starting transfers between devices, hop(): return lax.ppermute(x, axis, [(0, 1), (1, 0)])  23.5 us
    ppermute x23, waiting for transfers between devices, step(): return lax.ppermute(x, PLANE, ring_pairs(by, inner))  18 us
    pallas_call x4, Pallas kernels, project(): pl.pallas_call(project_kernel, grid=(1,), out_shape=jax.ShapeDtypeStruct(...  10.4 us
    pallas_call x2, Pallas kernels, attend(): pl.pallas_call(body, out_shape=jax.ShapeDtypeStruct((rows, columns * (1 +...  5.74 us
    unnamed x14, local copies, waits for them, and re-layouts  5.09 us
    pallas_call x6, Pallas kernels, partial_product(): pl.pallas_call(body, out_shape=jax.ShapeDtypeStruct((rows, columns), jnp....  4.8 us
  transfers between devices with their start and end apart: 27, of which 12 were waited for; matrix products, arithmetic and copies ran while one was open for 1% of the time, Pallas kernels for 17%

profile of v1, /device:TPU:2, one launch (start us, length us, event | category | flops | bytes accessed | tf_op | source)
XLA Modules:
  0.0 106.7 jit_solution(2232586281179817879)
XLA Ops:
  2.8 2.2 %collective-permute-start.13 = (bf16[128,4096]{1,0:T(8,128)(2,1)S(1)}, bf16[128,4096]{1,0:T(8,128)(2,1)S(1)}, u32[]{:S(2)}, u32[]{:S(2)}) collective-permute-start(bf16[128,4096]{1,0:T(8,128)(2,1)S(1)} %norm.1.own_ref), channel_id=1, source_target_pairs={{0,128},{128,0},{1,129},{129,1},{2,130},{130,2},{3,131},{131,3},{4... | collective-permute-start | bytes 3145736 | tf_op jit(solution)/shard_map/ppermute | solution.py:49
  7.0 3.9 %collective-permute-start.1 = (bf16[64,1024]{1,0:T(8,128)(2,1)}, bf16[64,1024]{1,0:T(8,128)(2,1)S(1)}, u32[]{:S(2)}, u32[]{:S(2)}) collective-permute-start(bf16[64,1024]{1,0:T(8,128)(2,1)} %refs_0_.1), channel_id=1, source_target_pairs={{0,7},{1,0},{2,1},{3,2},{4,3},{5,4},{6,5},{7,6},{16,23},{17,16},{1... | collective-permute-start | bytes 393224 | tf_op jit(solution)/shard_map/ppermute | solution.py:45
  10.9 3.2 %collective-permute-done.refs_1_ = bf16[64,1024]{1,0:T(8,128)(2,1)S(1)} collective-permute-done((bf16[64,1024]{1,0:T(8,128)(2,1)}, bf16[64,1024]{1,0:T(8,128)(2,1)S(1)}, u32[]{:S(2)}, u32[]{:S(2)}) %collective-permute-start) | collective-permute-done | bytes 131104 | tf_op jit(solution)/shard_map/ppermute | solution.py:45
  14.1 3.2 %collective-permute-start.3 = (bf16[64,1024]{1,0:T(8,128)(2,1)S(1)}, bf16[64,1024]{1,0:T(8,128)(2,1)S(1)}, u32[]{:S(2)}, u32[]{:S(2)}) collective-permute-start(bf16[64,1024]{1,0:T(8,128)(2,1)S(1)} %collective-permute-done.1.refs_2_), channel_id=1, source_target_pairs={{0,7},{1,0},{2,1},{3,2},{4,3},{5,4},{6,5},{7,6},{16,23},{17,16},{1... | collective-permute-start | bytes 393224 | tf_op jit(solution)/shard_map/ppermute | solution.py:45
  22.2 5.2 %collective-permute-start.6 = (bf16[64,1024]{1,0:T(8,128)(2,1)S(1)}, bf16[64,1024]{1,0:T(8,128)(2,1)S(1)}, u32[]{:S(2)}, u32[]{:S(2)}) collective-permute-start(bf16[64,1024]{1,0:T(8,128)(2,1)S(1)} %collective-permute-done.3.refs_4_), channel_id=1, source_target_pairs={{0,7},{1,0},{2,1},{3,2},{4,3},{5,4},{6,5},{7,6},{16,23},{17,16},{1... | collective-permute-start | bytes 393224 | tf_op jit(solution)/shard_map/ppermute | solution.py:45
  27.3 2.5 %collective-permute-done.6.refs_6_ = bf16[64,1024]{1,0:T(8,128)(2,1)S(1)} collective-permute-done((bf16[64,1024]{1,0:T(8,128)(2,1)S(1)}, bf16[64,1024]{1,0:T(8,128)(2,1)S(1)}, u32[]{:S(2)}, u32[]{:S(2)}) %collective-permute-start.6) | collective-permute-done | bytes 131104 | tf_op jit(solution)/shard_map/ppermute | solution.py:45
  29.9 3.7 %collective-permute-start.7 = (bf16[64,1024]{1,0:T(8,128)(2,1)S(1)}, bf16[64,1024]{1,0:T(8,128)(2,1)S(1)}, u32[]{:S(2)}, u32[]{:S(2)}) collective-permute-start(bf16[64,1024]{1,0:T(8,128)(2,1)S(1)} %collective-permute-done.6.refs_6_), channel_id=1, source_target_pairs={{0,7},{1,0},{2,1},{3,2},{4,3},{5,4},{6,5},{7,6},{16,23},{17,16},{1... | collective-permute-start | bytes 393224 | tf_op jit(solution)/shard_map/ppermute | solution.py:45
  37.2 2.0 %collective-permute-start.11 = (bf16[512,512]{1,0:T(8,128)(2,1)S(1)}, bf16[512,512]{1,0:T(8,128)(2,1)S(1)}, u32[]{:S(2)}, u32[]{:S(2)}) collective-permute-start(bf16[512,512]{1,0:T(8,128)(2,1)S(1)} %get-tuple-element.37.refs_0_), channel_id=1, source_target_pairs={{0,8},{1,9},{2,10},{3,11},{4,12},{5,13},{6,14},{7,15},{16,0},{17,1... | collective-permute-start | bytes 1572872 | tf_op jit(solution)/shard_map/ppermute | solution.py:45
  39.2 21.2 %collective-permute-start.14 = (bf16[128,4096]{1,0:T(8,128)(2,1)S(1)}, bf16[128,4096]{1,0:T(8,128)(2,1)S(1)}, u32[]{:S(2)}, u32[]{:S(2)}) collective-permute-start(bf16[128,4096]{1,0:T(8,128)(2,1)S(1)} %collective-permute-done.13.far_ref), channel_id=1, source_target_pairs={{0,64},{64,0},{1,65},{65,1},{2,66},{66,2},{3,67},{67,3},{4,68},{68... | collective-permute-start | bytes 3145736 | tf_op jit(solution)/shard_map/ppermute | solution.py:49
  60.4 2.0 %collective-permute-start.18 = (bf16[512,512]{1,0:T(8,128)(2,1)S(1)}, bf16[512,512]{1,0:T(8,128)(2,1)S(1)}, u32[]{:S(2)}, u32[]{:S(2)}) collective-permute-start(bf16[512,512]{1,0:T(8,128)(2,1)S(1)} %get-tuple-element.39.refs_0_), channel_id=1, source_target_pairs={{0,8},{1,9},{2,10},{3,11},{4,12},{5,13},{6,14},{7,15},{16,0},{17,1... | collective-permute-start | bytes 1572872 | tf_op jit(solution)/shard_map/ppermute | solution.py:45
  62.4 2.0 %copy-done.1 = bf16[2,896,1024]{2,1,0:T(8,128)(2,1)S(1)} copy-done((bf16[2,896,1024]{2,1,0:T(8,128)(2,1)S(1)}, bf16[2,896,1024]{2,1,0:T(8,128)(2,1)}, u32[]{:S(2)}) %copy-start.1) | copy-done | bytes 3670040
  64.4 2.6 %project.4.k_ref = bf16[9,256,512]{2,1,0:T(8,128)(2,1)S(1)} custom-call(bf16[1,256,896]{2,1,0:T(8,128)(2,1)S(1)} %collective-permute-done.9.prev_ref, bf16[8,256,896]{2,1,0:T(8,128)(2,1)S(1)} %copy-done, bf16[2,896,1024]{2,1,0:T(8,128)(2,1)S(1)} %copy-done.1), custom_call_target="tpu_custom_call" | custom-call | flops 2113929216 | bytes 6291456 | tf_op jit(solution)/shard_map/project/pallas_call | solution.py:151
  67.0 2.6 %project.5.v_ref = bf16[9,256,512]{2,1,0:T(8,128)(2,1)S(1)} custom-call(bf16[1,256,896]{2,1,0:T(8,128)(2,1)S(1)} %collective-permute-done.9.prev_ref, bf16[8,256,896]{2,1,0:T(8,128)(2,1)S(1)} %copy-done, bf16[2,896,1024]{2,1,0:T(8,128)(2,1)S(1)} %copy-done.1), custom_call_target="tpu_custom_call" | custom-call | flops 2113929216 | bytes 6291456 | tf_op jit(solution)/shard_map/project/pallas_call | solution.py:151
  69.8 2.0 %collective-permute-start.12 = (bf16[512,512]{1,0:T(8,128)(2,1)S(1)}, bf16[512,512]{1,0:T(8,128)(2,1)S(1)}, u32[]{:S(2)}, u32[]{:S(2)}) collective-permute-start(bf16[512,512]{1,0:T(8,128)(2,1)S(1)} %collective-permute-done.11.refs_2_), channel_id=1, source_target_pairs={{0,8},{1,9},{2,10},{3,11},{4,12},{5,13},{6,14},{7,15},{16,0},{17,1... | collective-permute-start | bytes 1572872 | tf_op jit(solution)/shard_map/ppermute | solution.py:45
  71.8 2.6 %project.6.k_ref = bf16[9,256,512]{2,1,0:T(8,128)(2,1)S(1)} custom-call(bf16[1,256,896]{2,1,0:T(8,128)(2,1)S(1)} %collective-permute-done.9.prev_ref, bf16[8,256,896]{2,1,0:T(8,128)(2,1)S(1)} %copy-done, bf16[2,896,1024]{2,1,0:T(8,128)(2,1)S(1)} %copy-done.1), custom_call_target="tpu_custom_call" | custom-call | flops 2113929216 | bytes 6291456 | tf_op jit(solution)/shard_map/project/pallas_call | solution.py:151
  74.6 1.9 %collective-permute-start.19 = (bf16[512,512]{1,0:T(8,128)(2,1)S(1)}, bf16[512,512]{1,0:T(8,128)(2,1)S(1)}, u32[]{:S(2)}, u32[]{:S(2)}) collective-permute-start(bf16[512,512]{1,0:T(8,128)(2,1)S(1)} %collective-permute-done.18.refs_2_), channel_id=1, source_target_pairs={{0,8},{1,9},{2,10},{3,11},{4,12},{5,13},{6,14},{7,15},{16,0},{17,1... | collective-permute-start | bytes 1572872 | tf_op jit(solution)/shard_map/ppermute | solution.py:45
  76.5 2.6 %project.7.v_ref = bf16[9,256,512]{2,1,0:T(8,128)(2,1)S(1)} custom-call(bf16[1,256,896]{2,1,0:T(8,128)(2,1)S(1)} %collective-permute-done.9.prev_ref, bf16[8,256,896]{2,1,0:T(8,128)(2,1)S(1)} %copy-done, bf16[2,896,1024]{2,1,0:T(8,128)(2,1)S(1)} %copy-done.1), custom_call_target="tpu_custom_call" | custom-call | flops 2113929216 | bytes 6291456 | tf_op jit(solution)/shard_map/project/pallas_call | solution.py:151
  79.3 1.9 %collective-permute-start.22 = (bf16[512,512]{1,0:T(8,128)(2,1)S(1)}, bf16[512,512]{1,0:T(8,128)(2,1)S(1)}, u32[]{:S(2)}, u32[]{:S(2)}) collective-permute-start(bf16[512,512]{1,0:T(8,128)(2,1)S(1)} %collective-permute-done.12.refs_1_), channel_id=1, source_target_pairs={{0,8},{1,9},{2,10},{3,11},{4,12},{5,13},{6,14},{7,15},{16,0},{17,1... | collective-permute-start | bytes 1572872 | tf_op jit(solution)/shard_map/ppermute | solution.py:45
  84.6 1.9 %collective-permute-start.20 = (bf16[512,512]{1,0:T(8,128)(2,1)S(1)}, bf16[512,512]{1,0:T(8,128)(2,1)S(1)}, u32[]{:S(2)}, u32[]{:S(2)}) collective-permute-start(bf16[512,512]{1,0:T(8,128)(2,1)S(1)} %collective-permute-done.19.refs_1_), channel_id=1, source_target_pairs={{0,8},{1,9},{2,10},{3,11},{4,12},{5,13},{6,14},{7,15},{16,0},{17,1... | collective-permute-start | bytes 1572872 | tf_op jit(solution)/shard_map/ppermute | solution.py:45
  90.3 2.1 %collective-permute-start.24 = (bf16[256,512]{1,0:T(8,128)(2,1)S(1)}, bf16[256,512]{1,0:T(8,128)(2,1)S(1)}, u32[]{:S(2)}, u32[]{:S(2)}) collective-permute-start(bf16[256,512]{1,0:T(8,128)(2,1)S(1)} %slice.21), channel_id=1, source_target_pairs={{0,8},{1,9},{2,10},{3,11},{4,12},{5,13},{6,14},{7,15},{16,0},{17,1... | collective-permute-start | bytes 786440 | tf_op jit(solution)/shard_map/ppermute | solution.py:45
  92.4 3.4 %collective-permute-done.17.refs_0_ = bf16[512,512]{1,0:T(8,128)(2,1)S(1)} collective-permute-done((bf16[512,512]{1,0:T(8,128)(2,1)S(1)}, bf16[512,512]{1,0:T(8,128)(2,1)S(1)}, u32[]{:S(2)}, u32[]{:S(2)}) %collective-permute-start.17) | collective-permute-done | bytes 524320 | tf_op jit(solution)/shard_map/ppermute | solution.py:45
  96.8 2.1 %collective-permute-start.26 = (bf16[256,512]{1,0:T(8,128)(2,1)S(1)}, bf16[256,512]{1,0:T(8,128)(2,1)S(1)}, u32[]{:S(2)}, u32[]{:S(2)}) collective-permute-start(bf16[256,512]{1,0:T(8,128)(2,1)S(1)} %slice.23), channel_id=1, source_target_pairs={{0,8},{1,9},{2,10},{3,11},{4,12},{5,13},{6,14},{7,15},{16,0},{17,1... | collective-permute-start | bytes 786440 | tf_op jit(solution)/shard_map/ppermute | solution.py:45
  99.6 2.3 %attend.2.refs_2_ = bf16[512,512]{1,0:T(8,128)(2,1)S(1)} custom-call(s32[2,512]{1,0:T(2,128)S(1)} %bitcast.6, s32[256,128]{1,0:T(8,128)S(1)} %bitcast.3, f32[512,512]{1,0:T(8,128)S(1)} %partial.10.total_ref, bf16[512,4096]{1,0:T(8,128)(2,1)S(1)} %rows.1.n_ref, bf16[9,256,512]{2,1,0:T(8,128)(2,1)S(1)} %project.4.k_ref, ...), custom_call_target="tpu_custom_call" | custom-call | flops 3145728000 | bytes 8388608 | tf_op jit(solution)/shard_map/attend/pallas_call | solution.py:272
  103.2 3.4 %attend.3 = bf16[512,1024]{1,0:T(8,128)(2,1)} custom-call(s32[2,512]{1,0:T(2,128)S(1)} %bitcast.7, s32[256,128]{1,0:T(8,128)S(1)} %bitcast.4, f32[512,512]{1,0:T(8,128)S(1)} %partial.11.total_ref, bf16[512,4096]{1,0:T(8,128)(2,1)S(1)} %rows.1.n_ref, bf16[9,256,512]{2,1,0:T(8,128)(2,1)S(1)} %project.6.k_ref, bf16[9,256,512]{2,1,0:T(8,128)(2,1)S(1)} %project.7.v_ref, ...), custom_call_target="tpu_custom_call" | custom-call | flops 3145728000 | bytes 8388608 | tf_op jit(solution)/shard_map/attend/pallas_call | solution.py:272
  (64 shorter events, 23.7 us)
Async XLA Ops:
  2.7 19.4 %collective-permute-start.4 = (bf16[128,4096]{1,0:T(8,128)(2,1)S(1)}, bf16[128,4096]{1,0:T(8,128)(2,1)S(1)}, u32[]{:S(2)}, u32[]{:S(2)}) collective-permute-start(bf16[128,4096]{1,0:T(8,128)(2,1)S(1)} %norm.1.own_ref), channel_id=1, source_target_pairs={{0,64},{64,0},{1,65},{65,1},{2,66},{66,2},{3,67},{67,3},{4,68},{68... | collective-permute-start | bytes 3145736 | tf_op jit(solution)/shard_map/ppermute | solution.py:49
  2.8 36.4 %collective-permute-start.13 = (bf16[128,4096]{1,0:T(8,128)(2,1)S(1)}, bf16[128,4096]{1,0:T(8,128)(2,1)S(1)}, u32[]{:S(2)}, u32[]{:S(2)}) collective-permute-start(bf16[128,4096]{1,0:T(8,128)(2,1)S(1)} %norm.1.own_ref), channel_id=1, source_target_pairs={{0,128},{128,0},{1,129},{129,1},{2,130},{130,2},{3,131},{131,3},{4... | collective-permute-start | bytes 3145736 | tf_op jit(solution)/shard_map/ppermute | solution.py:49
  5.0 9.0 %collective-permute-start = (bf16[64,1024]{1,0:T(8,128)(2,1)}, bf16[64,1024]{1,0:T(8,128)(2,1)S(1)}, u32[]{:S(2)}, u32[]{:S(2)}) collective-permute-start(bf16[64,1024]{1,0:T(8,128)(2,1)} %refs_0_.1), channel_id=1, source_target_pairs={{0,1},{1,2},{2,3},{3,4},{4,5},{5,6},{6,7},{7,0},{16,17},{17,18},{1... | collective-permute-start | bytes 393224 | tf_op jit(solution)/shard_map/ppermute | solution.py:45
  7.0 7.1 %collective-permute-start.1 = (bf16[64,1024]{1,0:T(8,128)(2,1)}, bf16[64,1024]{1,0:T(8,128)(2,1)S(1)}, u32[]{:S(2)}, u32[]{:S(2)}) collective-permute-start(bf16[64,1024]{1,0:T(8,128)(2,1)} %refs_0_.1), channel_id=1, source_target_pairs={{0,7},{1,0},{2,1},{3,2},{4,3},{5,4},{6,5},{7,6},{16,23},{17,16},{1... | collective-permute-start | bytes 393224 | tf_op jit(solution)/shard_map/ppermute | solution.py:45
  20.2 40.1 %collective-permute-start.9 = (bf16[1,256,896]{2,1,0:T(8,128)(2,1)S(1)}, bf16[1,256,896]{2,1,0:T(8,128)(2,1)S(1)}, u32[]{:S(2)}, u32[]{:S(2)}) collective-permute-start(bf16[1,256,896]{2,1,0:T(8,128)(2,1)S(1)} %slice.15), channel_id=1, source_target_pairs={{0,1},{1,2},{2,3},{3,4},{4,5},{5,6},{6,7},{7,8},{8,9},{9,10},{10,1... | collective-permute-start | bytes 1376264 | tf_op jit(solution)/shard_map/ppermute | solution.py:301
  22.2 7.7 %collective-permute-start.6 = (bf16[64,1024]{1,0:T(8,128)(2,1)S(1)}, bf16[64,1024]{1,0:T(8,128)(2,1)S(1)}, u32[]{:S(2)}, u32[]{:S(2)}) collective-permute-start(bf16[64,1024]{1,0:T(8,128)(2,1)S(1)} %collective-permute-done.3.refs_4_), channel_id=1, source_target_pairs={{0,7},{1,0},{2,1},{3,2},{4,3},{5,4},{6,5},{7,6},{16,23},{17,16},{1... | collective-permute-start | bytes 393224 | tf_op jit(solution)/shard_map/ppermute | solution.py:45
  27.3 7.8 %collective-permute-start.5 = (bf16[64,1024]{1,0:T(8,128)(2,1)S(1)}, bf16[64,1024]{1,0:T(8,128)(2,1)S(1)}, u32[]{:S(2)}, u32[]{:S(2)}) collective-permute-start(bf16[64,1024]{1,0:T(8,128)(2,1)S(1)} %collective-permute-done.2.refs_3_), channel_id=1, source_target_pairs={{0,1},{1,2},{2,3},{3,4},{4,5},{5,6},{6,7},{7,0},{16,17},{17,18},{1... | collective-permute-start | bytes 393224 | tf_op jit(solution)/shard_map/ppermute | solution.py:45
  37.1 32.6 %collective-permute-start.8 = (bf16[512,512]{1,0:T(8,128)(2,1)S(1)}, bf16[512,512]{1,0:T(8,128)(2,1)S(1)}, u32[]{:S(2)}, u32[]{:S(2)}) collective-permute-start(bf16[512,512]{1,0:T(8,128)(2,1)S(1)} %get-tuple-element.37.refs_0_), channel_id=1, source_target_pairs={{0,16},{1,17},{2,18},{3,19},{4,20},{5,21},{6,22},{7,23},{16,32},{1... | collective-permute-start | bytes 1572872 | tf_op jit(solution)/shard_map/ppermute | solution.py:45
  37.2 32.6 %collective-permute-start.11 = (bf16[512,512]{1,0:T(8,128)(2,1)S(1)}, bf16[512,512]{1,0:T(8,128)(2,1)S(1)}, u32[]{:S(2)}, u32[]{:S(2)}) collective-permute-start(bf16[512,512]{1,0:T(8,128)(2,1)S(1)} %get-tuple-element.37.refs_0_), channel_id=1, source_target_pairs={{0,8},{1,9},{2,10},{3,11},{4,12},{5,13},{6,14},{7,15},{16,0},{17,1... | collective-permute-start | bytes 1572872 | tf_op jit(solution)/shard_map/ppermute | solution.py:45
  39.2 39.9 %collective-permute-start.14 = (bf16[128,4096]{1,0:T(8,128)(2,1)S(1)}, bf16[128,4096]{1,0:T(8,128)(2,1)S(1)}, u32[]{:S(2)}, u32[]{:S(2)}) collective-permute-start(bf16[128,4096]{1,0:T(8,128)(2,1)S(1)} %collective-permute-done.13.far_ref), channel_id=1, source_target_pairs={{0,64},{64,0},{1,65},{65,1},{2,66},{66,2},{3,67},{67,3},{4,68},{68... | collective-permute-start | bytes 3145736 | tf_op jit(solution)/shard_map/ppermute | solution.py:49
  60.4 14.0 %collective-permute-start.15 = (bf16[512,512]{1,0:T(8,128)(2,1)S(1)}, bf16[512,512]{1,0:T(8,128)(2,1)S(1)}, u32[]{:S(2)}, u32[]{:S(2)}) collective-permute-start(bf16[512,512]{1,0:T(8,128)(2,1)S(1)} %get-tuple-element.39.refs_0_), channel_id=1, source_target_pairs={{0,16},{1,17},{2,18},{3,19},{4,20},{5,21},{6,22},{7,23},{16,32},{1... | collective-permute-start | bytes 1572872 | tf_op jit(solution)/shard_map/ppermute | solution.py:45
  60.4 14.2 %collective-permute-start.18 = (bf16[512,512]{1,0:T(8,128)(2,1)S(1)}, bf16[512,512]{1,0:T(8,128)(2,1)S(1)}, u32[]{:S(2)}, u32[]{:S(2)}) collective-permute-start(bf16[512,512]{1,0:T(8,128)(2,1)S(1)} %get-tuple-element.39.refs_0_), channel_id=1, source_target_pairs={{0,8},{1,9},{2,10},{3,11},{4,12},{5,13},{6,14},{7,15},{16,0},{17,1... | collective-permute-start | bytes 1572872 | tf_op jit(solution)/shard_map/ppermute | solution.py:45
  69.7 9.4 %collective-permute-start.10 = (bf16[512,512]{1,0:T(8,128)(2,1)S(1)}, bf16[512,512]{1,0:T(8,128)(2,1)S(1)}, u32[]{:S(2)}, u32[]{:S(2)}) collective-permute-start(bf16[512,512]{1,0:T(8,128)(2,1)S(1)} %collective-permute-done.8.refs_1_), channel_id=1, source_target_pairs={{0,16},{1,17},{2,18},{3,19},{4,20},{5,21},{6,22},{7,23},{16,32},{1... | collective-permute-start | bytes 1572872 | tf_op jit(solution)/shard_map/ppermute | solution.py:45
  69.8 9.5 %collective-permute-start.12 = (bf16[512,512]{1,0:T(8,128)(2,1)S(1)}, bf16[512,512]{1,0:T(8,128)(2,1)S(1)}, u32[]{:S(2)}, u32[]{:S(2)}) collective-permute-start(bf16[512,512]{1,0:T(8,128)(2,1)S(1)} %collective-permute-done.11.refs_2_), channel_id=1, source_target_pairs={{0,8},{1,9},{2,10},{3,11},{4,12},{5,13},{6,14},{7,15},{16,0},{17,1... | collective-permute-start | bytes 1572872 | tf_op jit(solution)/shard_map/ppermute | solution.py:45
  74.4 10.1 %collective-permute-start.16 = (bf16[512,512]{1,0:T(8,128)(2,1)S(1)}, bf16[512,512]{1,0:T(8,128)(2,1)S(1)}, u32[]{:S(2)}, u32[]{:S(2)}) collective-permute-start(bf16[512,512]{1,0:T(8,128)(2,1)S(1)} %collective-permute-done.15.refs_1_), channel_id=1, source_target_pairs={{0,16},{1,17},{2,18},{3,19},{4,20},{5,21},{6,22},{7,23},{16,32},{1... | collective-permute-start | bytes 1572872 | tf_op jit(solution)/shard_map/ppermute | solution.py:45
  74.6 10.1 %collective-permute-start.19 = (bf16[512,512]{1,0:T(8,128)(2,1)S(1)}, bf16[512,512]{1,0:T(8,128)(2,1)S(1)}, u32[]{:S(2)}, u32[]{:S(2)}) collective-permute-start(bf16[512,512]{1,0:T(8,128)(2,1)S(1)} %collective-permute-done.18.refs_2_), channel_id=1, source_target_pairs={{0,8},{1,9},{2,10},{3,11},{4,12},{5,13},{6,14},{7,15},{16,0},{17,1... | collective-permute-start | bytes 1572872 | tf_op jit(solution)/shard_map/ppermute | solution.py:45
  79.1 11.0 %collective-permute-start.21 = (bf16[512,512]{1,0:T(8,128)(2,1)S(1)}, bf16[512,512]{1,0:T(8,128)(2,1)S(1)}, u32[]{:S(2)}, u32[]{:S(2)}) collective-permute-start(bf16[512,512]{1,0:T(8,128)(2,1)S(1)} %collective-permute-done.10.refs_0_), channel_id=1, source_target_pairs={{0,16},{1,17},{2,18},{3,19},{4,20},{5,21},{6,22},{7,23},{16,32},{1... | collective-permute-start | bytes 1572872 | tf_op jit(solution)/shard_map/ppermute | solution.py:45
  79.3 11.0 %collective-permute-start.22 = (bf16[512,512]{1,0:T(8,128)(2,1)S(1)}, bf16[512,512]{1,0:T(8,128)(2,1)S(1)}, u32[]{:S(2)}, u32[]{:S(2)}) collective-permute-start(bf16[512,512]{1,0:T(8,128)(2,1)S(1)} %collective-permute-done.12.refs_1_), channel_id=1, source_target_pairs={{0,8},{1,9},{2,10},{3,11},{4,12},{5,13},{6,14},{7,15},{16,0},{17,1... | collective-permute-start | bytes 1572872 | tf_op jit(solution)/shard_map/ppermute | solution.py:45
  84.5 11.2 %collective-permute-start.17 = (bf16[512,512]{1,0:T(8,128)(2,1)S(1)}, bf16[512,512]{1,0:T(8,128)(2,1)S(1)}, u32[]{:S(2)}, u32[]{:S(2)}) collective-permute-start(bf16[512,512]{1,0:T(8,128)(2,1)S(1)} %collective-permute-done.16.refs_0_), channel_id=1, source_target_pairs={{0,16},{1,17},{2,18},{3,19},{4,20},{5,21},{6,22},{7,23},{16,32},{1... | collective-permute-start | bytes 1572872 | tf_op jit(solution)/shard_map/ppermute | solution.py:45
  84.6 11.2 %collective-permute-start.20 = (bf16[512,512]{1,0:T(8,128)(2,1)S(1)}, bf16[512,512]{1,0:T(8,128)(2,1)S(1)}, u32[]{:S(2)}, u32[]{:S(2)}) collective-permute-start(bf16[512,512]{1,0:T(8,128)(2,1)S(1)} %collective-permute-done.19.refs_1_), channel_id=1, source_target_pairs={{0,8},{1,9},{2,10},{3,11},{4,12},{5,13},{6,14},{7,15},{16,0},{17,1... | collective-permute-start | bytes 1572872 | tf_op jit(solution)/shard_map/ppermute | solution.py:45
  90.2 9.4 %collective-permute-start.23 = (bf16[256,512]{1,0:T(8,128)(2,1)S(1)}, bf16[256,512]{1,0:T(8,128)(2,1)S(1)}, u32[]{:S(2)}, u32[]{:S(2)}) collective-permute-start(bf16[256,512]{1,0:T(8,128)(2,1)S(1)} %slice.20), channel_id=1, source_target_pairs={{0,16},{1,17},{2,18},{3,19},{4,20},{5,21},{6,22},{7,23},{16,32},{1... | collective-permute-start | bytes 786440 | tf_op jit(solution)/shard_map/ppermute | solution.py:45
  90.3 9.3 %collective-permute-start.24 = (bf16[256,512]{1,0:T(8,128)(2,1)S(1)}, bf16[256,512]{1,0:T(8,128)(2,1)S(1)}, u32[]{:S(2)}, u32[]{:S(2)}) collective-permute-start(bf16[256,512]{1,0:T(8,128)(2,1)S(1)} %slice.21), channel_id=1, source_target_pairs={{0,8},{1,9},{2,10},{3,11},{4,12},{5,13},{6,14},{7,15},{16,0},{17,1... | collective-permute-start | bytes 786440 | tf_op jit(solution)/shard_map/ppermute | solution.py:45
  96.6 6.4 %collective-permute-start.25 = (bf16[256,512]{1,0:T(8,128)(2,1)S(1)}, bf16[256,512]{1,0:T(8,128)(2,1)S(1)}, u32[]{:S(2)}, u32[]{:S(2)}) collective-permute-start(bf16[256,512]{1,0:T(8,128)(2,1)S(1)} %slice.22), channel_id=1, source_target_pairs={{0,16},{1,17},{2,18},{3,19},{4,20},{5,21},{6,22},{7,23},{16,32},{1... | collective-permute-start | bytes 786440 | tf_op jit(solution)/shard_map/ppermute | solution.py:45
  96.8 6.4 %collective-permute-start.26 = (bf16[256,512]{1,0:T(8,128)(2,1)S(1)}, bf16[256,512]{1,0:T(8,128)(2,1)S(1)}, u32[]{:S(2)}, u32[]{:S(2)}) collective-permute-start(bf16[256,512]{1,0:T(8,128)(2,1)S(1)} %slice.23), channel_id=1, source_target_pairs={{0,8},{1,9},{2,10},{3,11},{4,12},{5,13},{6,14},{7,15},{16,0},{17,1... | collective-permute-start | bytes 786440 | tf_op jit(solution)/shard_map/ppermute | solution.py:45
  (10 other events, 91.7 us)

commit v2 on v1

v2 whole, which is shorter than its diff:
```python
import jax
import jax.numpy as jnp
from jax import lax
from jax.experimental import pallas as pl
from jax.experimental.pallas import tpu as pltpu
from jax.sharding import Mesh, PartitionSpec as P

HEAD_DIM = 128
SPAN = 64
NBR_LEN = 128
SIZES = {"xh": 2, "core": 2, "y": 4, "xl": 2, "z": 8}
PLANE = ("core", "y", "xl", "z")
VMEM = pl.BlockSpec(memory_space=pltpu.VMEM)
SMEM = pl.BlockSpec(memory_space=pltpu.SMEM)
MIB = 1 << 20


def params(mib):
    return pltpu.CompilerParams(vmem_limit_bytes=mib * MIB)


def cost(flops, moved, exps=0):
    return pl.CostEstimate(flops=flops, bytes_accessed=moved, transcendentals=exps)


def moved(move, y, xl, z):
    by, how = move
    if how == "z":
        return y, xl, (z + by) % 8
    return (y + by) % 4, xl ^ how, z


def send(x, first, second):
    pairs = []
    for core, move in enumerate((first, second)):
        for y in range(4):
            for xl in range(2):
                for z in range(8):
                    y2, xl2, z2 = moved(move, y, xl, z)
                    pairs.append(
                        (((core * 4 + y) * 2 + xl) * 8 + z, ((core * 4 + y2) * 2 + xl2) * 8 + z2)
                    )
    return lax.ppermute(x, PLANE, pairs)


def hop(x, axis):
    return lax.ppermute(x, axis, [(0, 1), (1, 0)])


INNER_Z = (0, -1, 1, -2, 2, -3, 3, -4)
INNER_W = ((0, 0), (0, 1), (-1, 0), (1, 0), (2, 0), (-1, 1), (1, 1), (2, 1))
OUTER_Z = (0, -1, 1, -2, 2, -3, 3, -4)
OUTER_W = ((0, 0), (-1, 0), (1, 0), (0, 1), (2, 0), (-1, 1), (1, 1), (2, 1))


def slots(on_z, by_z, by_w):
    y, xl, z = lax.axis_index("y"), lax.axis_index("xl"), lax.axis_index("z")
    out = []
    for dz, (dy, flip) in zip(by_z, by_w, strict=True):
        other = jnp.where(xl == flip, 0, 1)
        out.append(jnp.where(on_z, lax.rem(z + dz + 8, 8), lax.rem(y + dy + 4, 4) * 2 + other))
    return out


def stack_kernel(*refs):
    out, rows = refs[-1], refs[0].shape[0]
    places = slots(lax.axis_index("core") == 0, INNER_Z, INNER_W)
    for slot, ref in zip(places, refs[:-1], strict=True):
        out[pl.ds(pl.multiple_of(slot * rows, rows), rows), :] = ref[...]


def stacked(parts):
    rows, columns = parts[0].shape
    return pl.pallas_call(
        stack_kernel,
        out_shape=jax.ShapeDtypeStruct((8 * rows, columns), parts[0].dtype),
        in_specs=[VMEM] * 8,
        out_specs=VMEM,
        compiler_params=params(8),
        cost_estimate=cost(0, 32 * rows * columns),
        name="stack",
    )(*parts)


def norm_kernel(hidden_ref, gain_ref, out_ref):
    values = hidden_ref[...].astype(jnp.float32)
    factor = lax.rsqrt(jnp.mean(values * values, axis=-1, keepdims=True) + 1e-06)
    out_ref[...] = (values * factor * gain_ref[...]).astype(jnp.bfloat16)


def normalize(hidden, gain):
    rows, width = hidden.shape
    return pl.pallas_call(
        norm_kernel,
        out_shape=jax.ShapeDtypeStruct((rows, width), jnp.bfloat16),
        in_specs=[VMEM, VMEM],
        out_specs=VMEM,
        compiler_params=params(8),
        cost_estimate=cost(6 * rows * width, 4 * rows * width),
        name="norm",
    )(hidden, gain)


def rows_kernel(own_ref, near_ref, far_ref, far_near_ref, out):
    xh, core = lax.axis_index("xh"), lax.axis_index("core")
    slots = [xh * 2 + core, xh * 2 + 1 - core, 2 - 2 * xh + core, 3 - 2 * xh - core]
    refs = [own_ref, near_ref, far_ref, far_near_ref]
    rows = own_ref.shape[0]

    @pl.when(core == 0)
    def _():
        for slot, ref in zip(slots, refs, strict=True):
            out[pl.ds(pl.multiple_of(slot * rows, rows), rows), :] = ref[...]

    @pl.when(core == 1)
    def _():
        for slot, ref in zip(slots, refs, strict=True):
            at = pl.ds(pl.multiple_of(slot * rows, rows), rows)
            for z in range(8):
                for k in range(4):
                    one = ref[:, (16 * k + z) * 64 : (16 * k + z) * 64 + 64]
                    two = ref[:, (16 * k + 8 + z) * 64 : (16 * k + 8 + z) * 64 + 64]
                    to = z * 512 + k * 128
                    out[at, to : to + 128] = jnp.concatenate([one, two], axis=1)


def gather_rows(parts):
    rows, width = parts[0].shape
    return pl.pallas_call(
        rows_kernel,
        out_shape=jax.ShapeDtypeStruct((4 * rows, width), parts[0].dtype),
        in_specs=[VMEM] * 4,
        out_specs=VMEM,
        compiler_params=params(16),
        cost_estimate=cost(0, 16 * rows * width),
        name="rows",
    )(*parts)


def project_kernel(mine_ref, other_ref, states_ref, w_ref, out_ref):
    core, rows = lax.axis_index("core"), mine_ref.shape[0]
    for slot, ref in ((core, mine_ref), (1 - core, other_ref)):
        out_ref[0, pl.ds(pl.multiple_of(slot * rows, rows), rows), :] = jnp.dot(
            ref[...], w_ref[0], preferred_element_type=jnp.float32
        ).astype(jnp.bfloat16)
    for i in range(1, out_ref.shape[0]):
        out_ref[i] = jnp.dot(
            states_ref[i - 1], w_ref[0], preferred_element_type=jnp.float32
        ).astype(jnp.bfloat16)


def project(prev, states, w, which, half):
    spans, keys, depth = states.shape
    columns = w.shape[2] // 2
    whole = lambda i: (0, 0, 0)
    part = pl.BlockSpec(prev[0].shape, lambda i: (0, 0), pipeline_mode=pl.Buffered(1))
    return pl.pallas_call(
        project_kernel,
        grid=(1,),
        out_shape=jax.ShapeDtypeStruct((spans + 1, keys, columns), jnp.bfloat16),
        in_specs=[
            part,
            part,
            pl.BlockSpec(states.shape, whole, pipeline_mode=pl.Buffered(1)),
            pl.BlockSpec((1, depth, columns), lambda i: (which, 0, half), pipeline_mode=pl.Buffered(1)),
        ],
        out_specs=pl.BlockSpec((spans + 1, keys, columns), whole, pipeline_mode=pl.Buffered(1)),
        compiler_params=params(16),
        cost_estimate=cost(2 * (spans + 1) * keys * depth * columns, 6 * MIB),
        name="project",
    )(*prev, states, w)


def outer_slots(which):
    places = slots(lax.axis_index("core") == 1, OUTER_Z, OUTER_W)
    return [places[i] for i in which]


def products(n_ref, refs, places):
    total = None
    for ref, (slot, start) in zip(refs, places, strict=True):
        depth = ref.shape[0]
        lanes = pl.ds(pl.multiple_of(slot * 512 + start, 256), depth)
        term = jnp.dot(n_ref[:, lanes], ref[...], preferred_element_type=jnp.float32)
        total = term if total is None else total + term
    return total


def partial_product(n, which, pieces, before=None):
    rows, columns = n.shape[0], pieces[0].shape[1]
    depth = sum(p.shape[0] for p in pieces)
    extra = [] if before is None else [before]

    def body(n_ref, *refs):
        places = [(slot, 0) for slot in outer_slots(which)]
        total = products(n_ref, refs[: len(pieces)], places)
        if extra:
            total = total + refs[len(pieces)][...]
        refs[-1][...] = total

    return pl.pallas_call(
        body,
        out_shape=jax.ShapeDtypeStruct((rows, columns), jnp.float32),
        in_specs=[VMEM] * (1 + len(pieces) + len(extra)),
        out_specs=VMEM,
        compiler_params=params(16),
        cost_estimate=cost(2 * rows * depth * columns, 2 * depth * (rows + columns)),
        name="partial",
    )(n, *pieces, *extra)


def attend(lens, segments, total, n, pieces, keys, values):
    rows, columns = total.shape
    blocks = keys[0].shape[0]
    heads = columns // HEAD_DIM // 2
    half = columns // 2

    def body(lens_ref, seg_ref, total_ref, n_ref, one_ref, two_ref, *refs):
        k_refs, v_refs, (out_ref, q_scr, c_scr, s_scr, w_scr) = refs[:2], refs[2:4], refs[4:]
        seq = (lax.axis_index("y") * 2 + lax.axis_index("xl")) * 8 + lax.axis_index("z")
        (slot,) = outer_slots([7])
        acc = total_ref[...] + products(n_ref, [one_ref, two_ref], [(slot, 0), (slot, 256)])
        acc = acc * HEAD_DIM ** (-0.5)
        acc = jnp.concatenate([acc, jnp.zeros((SPAN, columns), jnp.float32)], axis=0)
        q_scr[...] = pltpu.roll(acc, 1, 0).astype(jnp.bfloat16)
        lane = lax.broadcasted_iota(jnp.int32, (1, 128), 1)
        wide = lax.broadcasted_iota(jnp.int32, (1, 2 * NBR_LEN), 1)
        row = lax.broadcasted_iota(jnp.int32, (SPAN, HEAD_DIM), 0)
        usable, live = [], []
        for b in range(blocks):
            span = jnp.maximum(seq * (blocks - 1) + b - 1, 0)
            usable.append(
                wide < jnp.where(wide < NBR_LEN, lens_ref[0, span], lens_ref[1, span] + NBR_LEN)
            )
            line = seg_ref[pl.ds(span // 2, 1), :]
            if b % 2:
                same = (line == line[:, 63:64]) & (lane >= 63) & (lane < 127)
                count = jnp.sum(same.astype(jnp.int32), axis=1, keepdims=True)
            else:
                after = seg_ref[pl.ds(jnp.minimum(span // 2 + 1, seg_ref.shape[0] - 1), 1), :]
                same = (after == line[:, 127:128]) & (lane < 63)
                count = jnp.sum(same.astype(jnp.int32), axis=1, keepdims=True) + 1
            if b == 0:
                count = jnp.where(seq == 0, 0, count)
            live.append(row < count)
        for part in range(2):
            for h in range(heads):
                at = slice(h * HEAD_DIM, (h + 1) * HEAD_DIM)
                to = slice(part * half + h * HEAD_DIM, part * half + (h + 1) * HEAD_DIM)
                for b in range(blocks):
                    scores = lax.dot_general(
                        q_scr[b * SPAN : (b + 1) * SPAN, to],
                        k_refs[part][b, :, at],
                        (((1,), (1,)), ((), ())),
                        preferred_element_type=jnp.float32,
                    )
                    s_scr[h, b * SPAN : (b + 1) * SPAN, :] = jnp.where(usable[b], scores, jnp.float32(-1e30))
            for h in range(heads):
                for c in range(blocks // 3):
                    r = slice(c * 3 * SPAN, (c + 1) * 3 * SPAN)
                    scores = s_scr[h, r, :]
                    weights = jnp.exp(scores - jnp.max(scores, axis=-1, keepdims=True))
                    scale = 1.0 / jnp.sum(weights, axis=-1, keepdims=True)
                    w_scr[h, r, :] = (weights * scale).astype(jnp.bfloat16)
            for h in range(heads):
                at = slice(h * HEAD_DIM, (h + 1) * HEAD_DIM)
                to = slice(part * half + h * HEAD_DIM, part * half + (h + 1) * HEAD_DIM)
                for b in range(blocks):
                    mixed = jnp.dot(
                        w_scr[h, b * SPAN : (b + 1) * SPAN, :],
                        v_refs[part][b, :, at],
                        preferred_element_type=jnp.float32,
                    )
                    c_scr[b * SPAN : (b + 1) * SPAN, to] = jnp.where(live[b], mixed, 0.0)
        moved = pltpu.roll(c_scr[...], blocks * SPAN - 1, 0)
        out_ref[...] = moved[:rows].astype(jnp.bfloat16)

    return pl.pallas_call(
        body,
        out_shape=jax.ShapeDtypeStruct((rows, columns), jnp.bfloat16),
        in_specs=[SMEM] + [VMEM] * 9,
        out_specs=VMEM,
        scratch_shapes=[
            pltpu.VMEM((blocks * SPAN, columns), jnp.bfloat16),
            pltpu.VMEM((blocks * SPAN, columns), jnp.float32),
            pltpu.VMEM((heads, blocks * SPAN, 2 * NBR_LEN), jnp.float32),
            pltpu.VMEM((heads, blocks * SPAN, 2 * NBR_LEN), jnp.bfloat16),
        ],
        compiler_params=params(28),
        cost_estimate=cost(6 * MIB * 1000, 16 * MIB),
        name="attend",
    )(lens, segments, total, n, *pieces, *keys, *values)


def after(value, *others):
    return lax.optimization_barrier((value, *others))[0]


def local(hidden, norm_gain, w_query, w_keyval, nbr_states, nbr_lens, segment_ids):
    core = lax.axis_index("core")

    def pick(zero, one):
        return jnp.where(core == 0, zero, one)

    inner = [
        w_query,
        send(w_query, (1, "z"), (0, 1)),
        send(w_query, (-1, "z"), (1, 0)),
        send(w_query, (2, "z"), (-1, 0)),
        send(w_query, (-2, "z"), (2, 0)),
    ]
    normed = normalize(hidden, norm_gain[None])
    near = hop(normed, "core")
    far = hop(normed, "xh")
    a = pick(inner[3], inner[1])
    b = pick(inner[4], inner[1])
    half = nbr_states.shape[1] // 2
    prev = lax.dynamic_slice_in_dim(nbr_states[-1], core * half, half, 0)
    prev = lax.ppermute(after(prev, a, b), ("y", "xl", "z"), [(i, i + 1) for i in range(63)])
    inner += [
        send(a, (1, "z"), (1, 0)),
        send(b, (-1, "z"), (-1, 0)),
        send(a, (2, "z"), (2, 0)),
    ]
    own = stacked([after(inner[0], prev), *inner[1:]])
    prev = [prev, hop(after(prev, own), "core")]

    def projected(which, part, *first):
        return project(prev, after(nbr_states, *first), w_keyval, which, part)

    outer = [own, send(own, (1, 0), (1, "z")), send(own, (-1, 0), (-1, "z"))]
    keys_a = projected(0, 0, own)
    far_near = hop(after(far, keys_a), "core")
    values_a = projected(1, 0, keys_a)
    first = after(outer[1], keys_a, values_a, far)
    outer += [
        send(pick(own, first), (0, 1), (1, "z")),
        send(after(outer[2], keys_a, values_a), (-1, 0), (-1, "z")),
    ]
    keys_b = projected(0, 1, *outer[1:3])
    values_b = projected(1, 1, keys_b)
    whole = gather_rows([after(normed, keys_b), near, far, far_near])
    outer += [
        send(after(outer[3], keys_b, values_b), (1, 0), (1, "z")),
        send(after(pick(outer[3], outer[4]), keys_b, values_b), (-1, 0), (-1, "z")),
    ]
    total = partial_product(after(whole, *outer[3:5]), [0, 1, 2], outer[:3])
    total = partial_product(whole, [3, 4], outer[3:5], total)
    r = own.shape[0] // 2
    last = [
        send(after(outer[5][:r], total), (1, 0), (1, "z")),
        send(after(outer[6][r:], total), (-1, 0), (-1, "z")),
    ]
    total = partial_product(whole, [5, 6], outer[5:7], total)
    return attend(
        nbr_lens.T,
        segment_ids.reshape(-1, 128),
        total,
        whole,
        last,
        [keys_a, keys_b],
        [values_a, values_b],
    )


def solution(mesh):
    fine = Mesh(mesh.devices.reshape(tuple(SIZES.values())), tuple(SIZES))
    section, seq = ("xh", "core"), ("y", "xl", "z")
    in_specs = (
        P(seq + section, None),
        P(),
        P(seq, section),
        P(None, None, section),
        P(seq, None, None),
        P(),
        P(),
    )
    out_specs = P(seq, section)
    return jax.shard_map(local, mesh=fine, in_specs=in_specs, out_specs=out_specs, check_vma=False)
```

time: 108 us -> 101 us (0.935)
  starting transfers between devices: 60 us -> 32.8 us
  waiting for transfers between devices: 18 us -> 40.7 us
  local copies, waits for them, and re-layouts: 6.22 us -> 3.94 us
    ppermute x24 -> x16, waiting for transfers between devices: 18 us -> 38.9 us  [the longest x15 38.3 us: send(): return lax.ppermute(x, PLANE, pairs)]
    ppermute x3 -> x4, starting transfers between devices: 23.5 us -> 2.64 us  [hop(): return lax.ppermute(x, axis, [(0, 1), (1, 0)])]
    ppermute x24 -> x16, starting transfers between devices: 36.5 us -> 30.2 us  [the longest x15 27.4 us: send(): return lax.ppermute(x, PLANE, pairs)]
    unnamed x14 -> x16, local copies, waits for them, and re-layouts: 5.09 us -> 2.79 us
    ppermute x3 -> x4, waiting for transfers between devices: 0.01 us -> 1.82 us  [hop(): return lax.ppermute(x, axis, [(0, 1), (1, 0)])]
    pallas_call x6 -> x3, Pallas kernels: 4.8 us -> 4.3 us  [partial_product(): pl.pallas_call(body, out_shape=jax.ShapeDtypeStruct((rows, columns), jnp....]
    pallas_call x3 -> x2, Pallas kernels: 5.87 us -> 6.12 us  [the longest x1 6.01 us: attend(): pl.pallas_call(body, out_shape=jax.ShapeDtypeStruct((rows, columns), jnp....]
  transfers between devices with their start and end apart: 27 -> 20, of which waited for: 12 -> 15; matrix products, arithmetic and copies ran while one was open for 1% -> 1% of each run, Pallas kernels for 17% -> 16%
where the time goes in v2:
time: 101 us; the launch traced here: 99.9 us
  waiting for transfers between devices  40.7 us (40%)
  starting transfers between devices  32.8 us (32%)
  Pallas kernels  22 us (22%)
  local copies, waits for them, and re-layouts  3.94 us (4%)
    ppermute x15, waiting for transfers between devices, send(): return lax.ppermute(x, PLANE, pairs)  38.3 us
    ppermute x15, starting transfers between devices, send(): return lax.ppermute(x, PLANE, pairs)  27.4 us
    pallas_call x4, Pallas kernels, project(): pl.pallas_call(project_kernel, grid=(1,), out_shape=jax.ShapeDtypeStruct(...  10.5 us
    pallas_call x1, Pallas kernels, attend(): pl.pallas_call(body, out_shape=jax.ShapeDtypeStruct((rows, columns), jnp....  6.01 us
    pallas_call x3, Pallas kernels, partial_product(): pl.pallas_call(body, out_shape=jax.ShapeDtypeStruct((rows, columns), jnp....  4.3 us
    unnamed x16, local copies, waits for them, and re-layouts  2.79 us
    ppermute x1, starting transfers between devices, local(): lax.ppermute(after(prev, a, b), ('y', 'xl', 'z'), [(i, i + 1) for i in ra...  2.75 us
    ppermute x4, starting transfers between devices, hop(): return lax.ppermute(x, axis, [(0, 1), (1, 0)])  2.64 us
  transfers between devices with their start and end apart: 20, of which 15 were waited for; matrix products, arithmetic and copies ran while one was open for 1% of the time, Pallas kernels for 16%

profile of v2, /device:TPU:2, one launch (start us, length us, event | category | flops | bytes accessed | tf_op | source)
XLA Modules:
  0.0 99.9 jit_solution(2260765639411443106)
XLA Ops:
  0.0 6.3 %collective-permute-start.2 = (bf16[64,1024]{1,0:T(8,128)(2,1)}, bf16[64,1024]{1,0:T(8,128)(2,1)S(1)}, u32[]{:S(2)}, u32[]{:S(2)}) collective-permute-start(bf16[64,1024]{1,0:T(8,128)(2,1)} %refs_0_), channel_id=1, source_target_pairs={{0,6},{1,7},{2,0},{3,1},{4,2},{5,3},{6,4},{7,5},{8,14},{9,15},{10,... | collective-permute-start | bytes 393224 | tf_op jit(solution)/shard_map/ppermute | solution.py:43
  8.4 2.1 %collective-permute-done.2.refs_4_ = bf16[64,1024]{1,0:T(8,128)(2,1)S(1)} collective-permute-done((bf16[64,1024]{1,0:T(8,128)(2,1)}, bf16[64,1024]{1,0:T(8,128)(2,1)S(1)}, u32[]{:S(2)}, u32[]{:S(2)}) %collective-permute-start.2) | collective-permute-done | bytes 131104 | tf_op jit(solution)/shard_map/ppermute | solution.py:43
  10.5 2.1 %collective-permute-done.1.refs_1_ = bf16[64,1024]{1,0:T(8,128)(2,1)S(1)} collective-permute-done((bf16[64,1024]{1,0:T(8,128)(2,1)}, bf16[64,1024]{1,0:T(8,128)(2,1)S(1)}, u32[]{:S(2)}, u32[]{:S(2)}) %collective-permute-start.1) | collective-permute-done | bytes 131104 | tf_op jit(solution)/shard_map/ppermute | solution.py:43
  12.7 3.3 %collective-permute-done.refs_3_ = bf16[64,1024]{1,0:T(8,128)(2,1)S(1)} collective-permute-done((bf16[64,1024]{1,0:T(8,128)(2,1)}, bf16[64,1024]{1,0:T(8,128)(2,1)S(1)}, u32[]{:S(2)}, u32[]{:S(2)}) %collective-permute-start) | collective-permute-done | bytes 131104 | tf_op jit(solution)/shard_map/ppermute | solution.py:43
  16.0 2.7 %collective-permute-start.3 = (bf16[128,896]{1,0:T(8,128)(2,1)S(1)}, bf16[128,896]{1,0:T(8,128)(2,1)S(1)}, u32[]{:S(2)}, u32[]{:S(2)}) collective-permute-start(bf16[128,896]{1,0:T(8,128)(2,1)S(1)} %dynamic-slice_bitcast_fusion), channel_id=1, source_target_pairs={{0,1},{1,2},{2,3},{3,4},{4,5},{5,6},{6,7},{7,8},{8,9},{9,10},{10,1... | collective-permute-start | bytes 688136 | tf_op jit(solution)/shard_map/ppermute | solution.py:319
  18.8 3.5 %collective-permute-start.4 = (bf16[64,1024]{1,0:T(8,128)(2,1)}, bf16[64,1024]{1,0:T(8,128)(2,1)S(1)}, u32[]{:S(2)}, u32[]{:S(2)}) collective-permute-start(bf16[64,1024]{1,0:T(8,128)(2,1)} %refs_0_), channel_id=1, source_target_pairs={{0,7},{1,0},{2,1},{3,2},{4,3},{5,4},{6,5},{7,6},{8,15},{9,8},{10,9... | collective-permute-start | bytes 393224 | tf_op jit(solution)/shard_map/ppermute | solution.py:43
  22.4 1.9 %collective-permute-start.5 = (bf16[64,1024]{1,0:T(8,128)(2,1)S(1)}, bf16[64,1024]{1,0:T(8,128)(2,1)S(1)}, u32[]{:S(2)}, u32[]{:S(2)}) collective-permute-start(bf16[64,1024]{1,0:T(8,128)(2,1)S(1)} %get-tuple-element.38), channel_id=1, source_target_pairs={{0,1},{1,2},{2,3},{3,4},{4,5},{5,6},{6,7},{7,0},{8,9},{9,10},{10,1... | collective-permute-start | bytes 393224 | tf_op jit(solution)/shard_map/ppermute | solution.py:43
  26.2 2.1 %collective-permute-start.12 = (bf16[128,4096]{1,0:T(8,128)(2,1)S(1)}, bf16[128,4096]{1,0:T(8,128)(2,1)S(1)}, u32[]{:S(2)}, u32[]{:S(2)}) collective-permute-start(bf16[128,4096]{1,0:T(8,128)(2,1)S(1)} %norm.1.own_ref), channel_id=1, source_target_pairs={{0,128},{128,0},{1,129},{129,1},{2,130},{130,2},{3,131},{131,3},{4... | collective-permute-start | bytes 3145736 | tf_op jit(solution)/shard_map/ppermute | solution.py:47
  28.6 2.2 %collective-permute-done.7.refs_7_ = bf16[64,1024]{1,0:T(8,128)(2,1)S(1)} collective-permute-done((bf16[64,1024]{1,0:T(8,128)(2,1)S(1)}, bf16[64,1024]{1,0:T(8,128)(2,1)S(1)}, u32[]{:S(2)}, u32[]{:S(2)}) %collective-permute-start.7) | collective-permute-done | bytes 131104 | tf_op jit(solution)/shard_map/ppermute | solution.py:43
  30.8 4.5 %collective-permute-done.5.refs_5_ = bf16[64,1024]{1,0:T(8,128)(2,1)S(1)} collective-permute-done((bf16[64,1024]{1,0:T(8,128)(2,1)S(1)}, bf16[64,1024]{1,0:T(8,128)(2,1)S(1)}, u32[]{:S(2)}, u32[]{:S(2)}) %collective-permute-start.5) | collective-permute-done | bytes 131104 | tf_op jit(solution)/shard_map/ppermute | solution.py:43
  35.5 1.9 %collective-permute-start.9 = (bf16[512,1024]{1,0:T(8,128)(2,1)S(1)}, bf16[512,1024]{1,0:T(8,128)(2,1)S(1)}, u32[]{:S(2)}, u32[]{:S(2)}) collective-permute-start(bf16[512,1024]{1,0:T(8,128)(2,1)S(1)} %stack.1.refs_0_), channel_id=1, source_target_pairs={{0,16},{1,17},{2,18},{3,19},{4,20},{5,21},{6,22},{7,23},{8,24},{9,... | collective-permute-start | bytes 3145736 | tf_op jit(solution)/shard_map/ppermute | solution.py:43
  40.3 2.0 %copy-done.1 = bf16[2,896,1024]{2,1,0:T(8,128)(2,1)S(1)} copy-done((bf16[2,896,1024]{2,1,0:T(8,128)(2,1)S(1)}, bf16[2,896,1024]{2,1,0:T(8,128)(2,1)}, u32[]{:S(2)}) %copy-start.1) | copy-done | bytes 3670040
  42.3 2.6 %project.5.refs_0_ = bf16[9,256,512]{2,1,0:T(8,128)(2,1)S(1)} custom-call(bf16[128,896]{1,0:T(8,128)(2,1)S(1)} %collective-permute-done.3.mine_ref, bf16[128,896]{1,0:T(8,128)(2,1)S(1)} %collective-permute-done.8.other_ref, bf16[8,256,896]{2,1,0:T(8,128)(2,1)S(1)} %copy-done, bf16[2,896,1024]{2,1,0:T(8,128)(2,1)S(1)} %copy-done.1), custom_call_target="tpu_custom_call" | custom-call | flops 2113929216 | bytes 6291456 | tf_op jit(solution)/shard_map/project/pallas_call | solution.py:157
  45.0 2.6 %project.6.refs_2_ = bf16[9,256,512]{2,1,0:T(8,128)(2,1)S(1)} custom-call(bf16[128,896]{1,0:T(8,128)(2,1)S(1)} %collective-permute-done.3.mine_ref, bf16[128,896]{1,0:T(8,128)(2,1)S(1)} %collective-permute-done.8.other_ref, bf16[8,256,896]{2,1,0:T(8,128)(2,1)S(1)} %copy-done, bf16[2,896,1024]{2,1,0:T(8,128)(2,1)S(1)} %copy-done.1), custom_call_target="tpu_custom_call" | custom-call | flops 2113929216 | bytes 6291456 | tf_op jit(solution)/shard_map/project/pallas_call | solution.py:157
  47.9 3.6 %collective-permute-done.9.refs_1_ = bf16[512,1024]{1,0:T(8,128)(2,1)S(1)} collective-permute-done((bf16[512,1024]{1,0:T(8,128)(2,1)S(1)}, bf16[512,1024]{1,0:T(8,128)(2,1)S(1)}, u32[]{:S(2)}, u32[]{:S(2)}) %collective-permute-start.9) | collective-permute-done | bytes 1048608 | tf_op jit(solution)/shard_map/ppermute | solution.py:43
  52.2 2.6 %collective-permute-start.16 = (bf16[512,1024]{1,0:T(8,128)(2,1)S(1)}, bf16[512,1024]{1,0:T(8,128)(2,1)S(1)}, u32[]{:S(2)}, u32[]{:S(2)}) collective-permute-start(bf16[512,1024]{1,0:T(8,128)(2,1)S(1)} %collective-permute-done.10.refs_2_), channel_id=1, source_target_pairs={{0,48},{1,49},{2,50},{3,51},{4,52},{5,53},{6,54},{7,55},{8,56},{9,... | collective-permute-start | bytes 3145736 | tf_op jit(solution)/shard_map/ppermute | solution.py:43
  55.3 2.6 %project.4.refs_1_ = bf16[9,256,512]{2,1,0:T(8,128)(2,1)S(1)} custom-call(bf16[128,896]{1,0:T(8,128)(2,1)S(1)} %collective-permute-done.3.mine_ref, bf16[128,896]{1,0:T(8,128)(2,1)S(1)} %collective-permute-done.8.other_ref, bf16[8,256,896]{2,1,0:T(8,128)(2,1)S(1)} %copy-done, bf16[2,896,1024]{2,1,0:T(8,128)(2,1)S(1)} %copy-done.2), custom_call_target="tpu_custom_call" | custom-call | flops 2113929216 | bytes 6291456 | tf_op jit(solution)/shard_map/project/pallas_call | solution.py:157
  57.9 2.6 %project.7.refs_3_ = bf16[9,256,512]{2,1,0:T(8,128)(2,1)S(1)} custom-call(bf16[128,896]{1,0:T(8,128)(2,1)S(1)} %collective-permute-done.3.mine_ref, bf16[128,896]{1,0:T(8,128)(2,1)S(1)} %collective-permute-done.8.other_ref, bf16[8,256,896]{2,1,0:T(8,128)(2,1)S(1)} %copy-done, bf16[2,896,1024]{2,1,0:T(8,128)(2,1)S(1)} %copy-done.2), custom_call_target="tpu_custom_call" | custom-call | flops 2113929216 | bytes 6291456 | tf_op jit(solution)/shard_map/project/pallas_call | solution.py:157
  60.6 6.0 %collective-permute-done.14.refs_0_ = bf16[512,1024]{1,0:T(8,128)(2,1)S(1)} collective-permute-done((bf16[512,1024]{1,0:T(8,128)(2,1)S(1)}, bf16[512,1024]{1,0:T(8,128)(2,1)S(1)}, u32[]{:S(2)}, u32[]{:S(2)}) %collective-permute-start.14) | collective-permute-done | bytes 1048608 | tf_op jit(solution)/shard_map/ppermute | solution.py:43
  67.3 3.7 %collective-permute-start.17 = (bf16[512,1024]{1,0:T(8,128)(2,1)S(1)}, bf16[512,1024]{1,0:T(8,128)(2,1)S(1)}, u32[]{:S(2)}, u32[]{:S(2)}) collective-permute-start(bf16[512,1024]{1,0:T(8,128)(2,1)S(1)} %broadcast_select_fusion), channel_id=1, source_target_pairs={{0,48},{1,49},{2,50},{3,51},{4,52},{5,53},{6,54},{7,55},{8,56},{9,... | collective-permute-start | bytes 3145736 | tf_op jit(solution)/shard_map/ppermute | solution.py:43
  74.6 8.0 %collective-permute-done.15.refs_0_ = bf16[512,1024]{1,0:T(8,128)(2,1)S(1)} collective-permute-done((bf16[512,1024]{1,0:T(8,128)(2,1)S(1)}, bf16[512,1024]{1,0:T(8,128)(2,1)S(1)}, u32[]{:S(2)}, u32[]{:S(2)}) %collective-permute-start.15) | collective-permute-done | bytes 1048608 | tf_op jit(solution)/shard_map/ppermute | solution.py:43
  83.4 3.8 %collective-permute-start.19 = (bf16[256,1024]{1,0:T(8,128)(2,1)S(1)}, bf16[256,1024]{1,0:T(8,128)(2,1)S(1)}, u32[]{:S(2)}, u32[]{:S(2)}) collective-permute-start(bf16[256,1024]{1,0:T(8,128)(2,1)S(1)} %slice.13), channel_id=1, source_target_pairs={{0,48},{1,49},{2,50},{3,51},{4,52},{5,53},{6,54},{7,55},{8,56},{9,... | collective-permute-start | bytes 1572872 | tf_op jit(solution)/shard_map/ppermute | solution.py:43
  88.4 4.7 %collective-permute-done.18.one_ref = bf16[256,1024]{1,0:T(8,128)(2,1)S(1)} collective-permute-done((bf16[256,1024]{1,0:T(8,128)(2,1)S(1)}, bf16[256,1024]{1,0:T(8,128)(2,1)S(1)}, u32[]{:S(2)}, u32[]{:S(2)}) %collective-permute-start.18) | collective-permute-done | bytes 524320 | tf_op jit(solution)/shard_map/ppermute | solution.py:43
  93.8 6.0 %attend.1 = bf16[512,1024]{1,0:T(8,128)(2,1)} custom-call(s32[2,512]{1,0:T(2,128)S(1)} %bitcast.7, s32[256,128]{1,0:T(8,128)S(1)} %bitcast.6, f32[512,1024]{1,0:T(8,128)S(1)} %partial.5.total_ref, bf16[512,4096]{1,0:T(8,128)(2,1)S(1)} %rows.1.n_ref, bf16[256,1024]{1,0:T(8,128)(2,1)S(1)} %collective-permute-done.18.one_ref, ...), custom_call_target="tpu_custom_call" | custom-call | flops 6291456000 | bytes 16777216 | tf_op jit(solution)/shard_map/attend/pallas_call | solution.py:278
  (50 shorter events, 16.0 us)
Async XLA Ops:
  0.0 35.3 %copy-start.4 = (bf16[64,1024]{1,0:T(8,128)(2,1)S(1)}, bf16[64,1024]{1,0:T(8,128)(2,1)}, u32[]{:S(2)}) copy-start(bf16[64,1024]{1,0:T(8,128)(2,1)} %refs_0_) | copy-start | bytes 393220
  0.0 24.3 %copy-start.3 = (bf16[128,4096]{1,0:T(8,128)(2,1)S(1)}, bf16[128,4096]{1,0:T(8,128)(2,1)}, u32[]{:S(2)}) copy-start(bf16[128,4096]{1,0:T(8,128)(2,1)} %hidden_ref.1) | copy-start | bytes 3145732
  0.0 10.5 %collective-permute-start.2 = (bf16[64,1024]{1,0:T(8,128)(2,1)}, bf16[64,1024]{1,0:T(8,128)(2,1)S(1)}, u32[]{:S(2)}, u32[]{:S(2)}) collective-permute-start(bf16[64,1024]{1,0:T(8,128)(2,1)} %refs_0_), channel_id=1, source_target_pairs={{0,6},{1,7},{2,0},{3,1},{4,2},{5,3},{6,4},{7,5},{8,14},{9,15},{10,... | collective-permute-start | bytes 393224 | tf_op jit(solution)/shard_map/ppermute | solution.py:43
  6.3 6.4 %collective-permute-start.1 = (bf16[64,1024]{1,0:T(8,128)(2,1)}, bf16[64,1024]{1,0:T(8,128)(2,1)S(1)}, u32[]{:S(2)}, u32[]{:S(2)}) collective-permute-start(bf16[64,1024]{1,0:T(8,128)(2,1)} %refs_0_), channel_id=1, source_target_pairs={{0,1},{1,2},{2,3},{3,4},{4,5},{5,6},{6,7},{7,0},{8,9},{9,10},{10,1... | collective-permute-start | bytes 393224 | tf_op jit(solution)/shard_map/ppermute | solution.py:43
  7.3 8.7 %collective-permute-start = (bf16[64,1024]{1,0:T(8,128)(2,1)}, bf16[64,1024]{1,0:T(8,128)(2,1)S(1)}, u32[]{:S(2)}, u32[]{:S(2)}) collective-permute-start(bf16[64,1024]{1,0:T(8,128)(2,1)} %refs_0_), channel_id=1, source_target_pairs={{0,2},{1,3},{2,4},{3,5},{4,6},{5,7},{6,0},{7,1},{8,10},{9,11},{10,... | collective-permute-start | bytes 393224 | tf_op jit(solution)/shard_map/ppermute | solution.py:43
  8.4 31.9 %copy-start = (bf16[8,256,896]{2,1,0:T(8,128)(2,1)S(1)}, bf16[8,256,896]{2,1,0:T(8,128)(2,1)}, u32[]{:S(2)}) copy-start(bf16[8,256,896]{2,1,0:T(8,128)(2,1)} %states_ref.3) | copy-start | bytes 11010052
  16.0 10.1 %collective-permute-start.3 = (bf16[128,896]{1,0:T(8,128)(2,1)S(1)}, bf16[128,896]{1,0:T(8,128)(2,1)S(1)}, u32[]{:S(2)}, u32[]{:S(2)}) collective-permute-start(bf16[128,896]{1,0:T(8,128)(2,1)S(1)} %dynamic-slice_bitcast_fusion), channel_id=1, source_target_pairs={{0,1},{1,2},{2,3},{3,4},{4,5},{5,6},{6,7},{7,8},{8,9},{9,10},{10,1... | collective-permute-start | bytes 688136 | tf_op jit(solution)/shard_map/ppermute | solution.py:319
  18.8 9.5 %collective-permute-start.4 = (bf16[64,1024]{1,0:T(8,128)(2,1)}, bf16[64,1024]{1,0:T(8,128)(2,1)S(1)}, u32[]{:S(2)}, u32[]{:S(2)}) collective-permute-start(bf16[64,1024]{1,0:T(8,128)(2,1)} %refs_0_), channel_id=1, source_target_pairs={{0,7},{1,0},{2,1},{3,2},{4,3},{5,4},{6,5},{7,6},{8,15},{9,8},{10,9... | collective-permute-start | bytes 393224 | tf_op jit(solution)/shard_map/ppermute | solution.py:43
  22.3 6.3 %collective-permute-start.6 = (bf16[64,1024]{1,0:T(8,128)(2,1)S(1)}, bf16[64,1024]{1,0:T(8,128)(2,1)S(1)}, u32[]{:S(2)}, u32[]{:S(2)}) collective-permute-start(bf16[64,1024]{1,0:T(8,128)(2,1)S(1)} %get-tuple-element.37), channel_id=1, source_target_pairs={{0,7},{1,0},{2,1},{3,2},{4,3},{5,4},{6,5},{7,6},{8,15},{9,8},{10,9... | collective-permute-start | bytes 393224 | tf_op jit(solution)/shard_map/ppermute | solution.py:43
  22.4 8.5 %collective-permute-start.7 = (bf16[64,1024]{1,0:T(8,128)(2,1)S(1)}, bf16[64,1024]{1,0:T(8,128)(2,1)S(1)}, u32[]{:S(2)}, u32[]{:S(2)}) collective-permute-start(bf16[64,1024]{1,0:T(8,128)(2,1)S(1)} %get-tuple-element.38), channel_id=1, source_target_pairs={{0,2},{1,3},{2,4},{3,5},{4,6},{5,7},{6,0},{7,1},{8,10},{9,11},{10,... | collective-permute-start | bytes 393224 | tf_op jit(solution)/shard_map/ppermute | solution.py:43
  22.4 13.0 %collective-permute-start.5 = (bf16[64,1024]{1,0:T(8,128)(2,1)S(1)}, bf16[64,1024]{1,0:T(8,128)(2,1)S(1)}, u32[]{:S(2)}, u32[]{:S(2)}) collective-permute-start(bf16[64,1024]{1,0:T(8,128)(2,1)S(1)} %get-tuple-element.38), channel_id=1, source_target_pairs={{0,1},{1,2},{2,3},{3,4},{4,5},{5,6},{6,7},{7,0},{8,9},{9,10},{10,1... | collective-permute-start | bytes 393224 | tf_op jit(solution)/shard_map/ppermute | solution.py:43
  26.2 21.7 %collective-permute-start.12 = (bf16[128,4096]{1,0:T(8,128)(2,1)S(1)}, bf16[128,4096]{1,0:T(8,128)(2,1)S(1)}, u32[]{:S(2)}, u32[]{:S(2)}) collective-permute-start(bf16[128,4096]{1,0:T(8,128)(2,1)S(1)} %norm.1.own_ref), channel_id=1, source_target_pairs={{0,128},{128,0},{1,129},{129,1},{2,130},{130,2},{3,131},{131,3},{4... | collective-permute-start | bytes 3145736 | tf_op jit(solution)/shard_map/ppermute | solution.py:47
  35.5 16.1 %collective-permute-start.9 = (bf16[512,1024]{1,0:T(8,128)(2,1)S(1)}, bf16[512,1024]{1,0:T(8,128)(2,1)S(1)}, u32[]{:S(2)}, u32[]{:S(2)}) collective-permute-start(bf16[512,1024]{1,0:T(8,128)(2,1)S(1)} %stack.1.refs_0_), channel_id=1, source_target_pairs={{0,16},{1,17},{2,18},{3,19},{4,20},{5,21},{6,22},{7,23},{8,24},{9,... | collective-permute-start | bytes 3145736 | tf_op jit(solution)/shard_map/ppermute | solution.py:43
  37.4 14.9 %collective-permute-start.10 = (bf16[512,1024]{1,0:T(8,128)(2,1)S(1)}, bf16[512,1024]{1,0:T(8,128)(2,1)S(1)}, u32[]{:S(2)}, u32[]{:S(2)}) collective-permute-start(bf16[512,1024]{1,0:T(8,128)(2,1)S(1)} %stack.1.refs_0_), channel_id=1, source_target_pairs={{0,48},{1,49},{2,50},{3,51},{4,52},{5,53},{6,54},{7,55},{8,56},{9,... | collective-permute-start | bytes 3145736 | tf_op jit(solution)/shard_map/ppermute | solution.py:43
  38.8 1.5 %collective-permute-start.8 = (bf16[128,896]{1,0:T(8,128)(2,1)S(1)}, bf16[128,896]{1,0:T(8,128)(2,1)S(1)}, u32[]{:S(2)}, u32[]{:S(2)}) collective-permute-start(bf16[128,896]{1,0:T(8,128)(2,1)S(1)} %collective-permute-done.3.mine_ref), channel_id=1, source_target_pairs={{0,64},{64,0},{1,65},{65,1},{2,66},{66,2},{3,67},{67,3},{4,68},{68... | collective-permute-start | bytes 688136 | tf_op jit(solution)/shard_map/ppermute | solution.py:47
  51.7 14.9 %collective-permute-start.14 = (bf16[512,1024]{1,0:T(8,128)(2,1)S(1)}, bf16[512,1024]{1,0:T(8,128)(2,1)S(1)}, u32[]{:S(2)}, u32[]{:S(2)}) collective-permute-start(bf16[512,1024]{1,0:T(8,128)(2,1)S(1)} %broadcast_select_fusion.1), channel_id=1, source_target_pairs={{0,8},{1,9},{2,10},{3,11},{4,12},{5,13},{6,14},{7,15},{8,0},{9,1},... | collective-permute-start | bytes 3145736 | tf_op jit(solution)/shard_map/ppermute | solution.py:43
  52.2 14.9 %collective-permute-start.16 = (bf16[512,1024]{1,0:T(8,128)(2,1)S(1)}, bf16[512,1024]{1,0:T(8,128)(2,1)S(1)}, u32[]{:S(2)}, u32[]{:S(2)}) collective-permute-start(bf16[512,1024]{1,0:T(8,128)(2,1)S(1)} %collective-permute-done.10.refs_2_), channel_id=1, source_target_pairs={{0,48},{1,49},{2,50},{3,51},{4,52},{5,53},{6,54},{7,55},{8,56},{9,... | collective-permute-start | bytes 3145736 | tf_op jit(solution)/shard_map/ppermute | solution.py:43
  54.8 16.2 %collective-permute-start.11 = (bf16[128,4096]{1,0:T(8,128)(2,1)S(1)}, bf16[128,4096]{1,0:T(8,128)(2,1)S(1)}, u32[]{:S(2)}, u32[]{:S(2)}) collective-permute-start(bf16[128,4096]{1,0:T(8,128)(2,1)S(1)} %norm.1.own_ref), channel_id=1, source_target_pairs={{0,64},{64,0},{1,65},{65,1},{2,66},{66,2},{3,67},{67,3},{4,68},{68... | collective-permute-start | bytes 3145736 | tf_op jit(solution)/shard_map/ppermute | solution.py:47
  54.8 16.2 %collective-permute-start.13 = (bf16[128,4096]{1,0:T(8,128)(2,1)S(1)}, bf16[128,4096]{1,0:T(8,128)(2,1)S(1)}, u32[]{:S(2)}, u32[]{:S(2)}) collective-permute-start(bf16[128,4096]{1,0:T(8,128)(2,1)S(1)} %collective-permute-done.12.far_ref), channel_id=1, source_target_pairs={{0,64},{64,0},{1,65},{65,1},{2,66},{66,2},{3,67},{67,3},{4,68},{68... | collective-permute-start | bytes 3145736 | tf_op jit(solution)/shard_map/ppermute | solution.py:47
  66.5 16.0 %collective-permute-start.15 = (bf16[512,1024]{1,0:T(8,128)(2,1)S(1)}, bf16[512,1024]{1,0:T(8,128)(2,1)S(1)}, u32[]{:S(2)}, u32[]{:S(2)}) collective-permute-start(bf16[512,1024]{1,0:T(8,128)(2,1)S(1)} %collective-permute-done.14.refs_0_), channel_id=1, source_target_pairs={{0,16},{1,17},{2,18},{3,19},{4,20},{5,21},{6,22},{7,23},{8,24},{9,... | collective-permute-start | bytes 3145736 | tf_op jit(solution)/shard_map/ppermute | solution.py:43
  67.3 16.0 %collective-permute-start.17 = (bf16[512,1024]{1,0:T(8,128)(2,1)S(1)}, bf16[512,1024]{1,0:T(8,128)(2,1)S(1)}, u32[]{:S(2)}, u32[]{:S(2)}) collective-permute-start(bf16[512,1024]{1,0:T(8,128)(2,1)S(1)} %broadcast_select_fusion), channel_id=1, source_target_pairs={{0,48},{1,49},{2,50},{3,51},{4,52},{5,53},{6,54},{7,55},{8,56},{9,... | collective-permute-start | bytes 3145736 | tf_op jit(solution)/shard_map/ppermute | solution.py:43
  82.6 10.5 %collective-permute-start.18 = (bf16[256,1024]{1,0:T(8,128)(2,1)S(1)}, bf16[256,1024]{1,0:T(8,128)(2,1)S(1)}, u32[]{:S(2)}, u32[]{:S(2)}) collective-permute-start(bf16[256,1024]{1,0:T(8,128)(2,1)S(1)} %slice.12), channel_id=1, source_target_pairs={{0,16},{1,17},{2,18},{3,19},{4,20},{5,21},{6,22},{7,23},{8,24},{9,... | collective-permute-start | bytes 1572872 | tf_op jit(solution)/shard_map/ppermute | solution.py:43
  83.3 10.5 %copy-start.6 = (s32[32768]{0:T(1024)S(1)}, s32[32768]{0:T(1024)}, u32[]{:S(2)}) copy-start(s32[32768]{0:T(1024)} %param.13) | copy-start | bytes 393220
  83.4 10.5 %collective-permute-start.19 = (bf16[256,1024]{1,0:T(8,128)(2,1)S(1)}, bf16[256,1024]{1,0:T(8,128)(2,1)S(1)}, u32[]{:S(2)}, u32[]{:S(2)}) collective-permute-start(bf16[256,1024]{1,0:T(8,128)(2,1)S(1)} %slice.13), channel_id=1, source_target_pairs={{0,48},{1,49},{2,50},{3,51},{4,52},{5,53},{6,54},{7,55},{8,56},{9,... | collective-permute-start | bytes 1572872 | tf_op jit(solution)/shard_map/ppermute | solution.py:43
  (4 other events, 23.6 us)
